TPU v7x, 128 devices: a whole 4x4x4 slice. The times are simulated.
128 devices in a mesh: sec: 4 (over x), fsdp: 4 (over y_hi, core), tp: 8 (over y_lo, z).
Axes of the slice: x: 4, y: 4 (y_hi: 2, y_lo: 2; y = y_hi * 2 + y_lo), z: 4, core: 2. Of those that a mesh axis runs over, the one named last changes fastest.
Arguments:
- layer_input: bfloat16 [65536, 5120], P(('sec', 'fsdp'), 'tp'), may hold values from -6 to 6
- value_cotangent: bfloat16 [65536, 1024], P(('sec', 'fsdp')), may hold values from -6 to 6
- value_weight: bfloat16 [1024, 5120], P(('sec', 'fsdp'), 'tp'), may hold values from -0.078125 to 0.078125
- rewards: float32 [64], replicated, may hold values from -3 to 3
- group_ids: int32 [64], replicated, may hold values from 0 to 7, as said below
- prompt_lengths: int32 [64], replicated, may hold values from 128 to 895
- step_inputs: bfloat16 [4, 64, 5120], P(None, ('sec', 'fsdp')), may hold values from -6 to 6
- queries: bfloat16 [4, 64, 8192], P(None, ('sec', 'fsdp'), 'tp'), may hold values from -24 to 24
- key_weight: bfloat16 [1024, 5120], P('tp'), may hold values from -0.078125 to 0.078125
- cache_keys: bfloat16 [64, 2048, 1024], P(('sec', 'fsdp'), None, 'tp'), may hold values from -6 to 6
- cache_values: bfloat16 [64, 2048, 1024], P(('sec', 'fsdp'), None, 'tp'), may hold values from -6 to 6
- cache_lengths: int32 [64], P(('sec', 'fsdp')), may hold values from 256 to 2048
Outputs:
- input_grad: bfloat16 [65536, 5120], P(('sec', 'fsdp'), 'tp')
- new_keys: bfloat16 [4, 64, 1024], P(None, ('sec', 'fsdp'), 'tp')
- new_values: bfloat16 [4, 64, 1024], P(None, ('sec', 'fsdp'), 'tp')
- attended: bfloat16 [4, 64, 8192], P(None, ('sec', 'fsdp'), 'tp')
Inputs may be any that keep to these rules, and one draw needn't show every extreme that they name: `group_ids`: each group id names exactly 8 sequences.
All inputs are finite; a program needn't handle non-finite values.
Results may differ from a plain program's by a relative error of at most 0.0052.
Values may be sent and summed in bfloat16 or wider, within the bound.
A program may use at most 128 MiB of HBM per device.

v0:
```python
import jax
import jax.numpy as jnp
from jax import lax
from jax.sharding import PartitionSpec as P

HEAD = 128
QPK = 8
SEQ_LEN = 1024
GROUP = 8


def body(
    layer_input,
    value_cotangent,
    value_weight,
    rewards,
    group_ids,
    prompt_lengths,
    step_inputs,
    queries,
    key_weight,
    cache_keys,
    cache_values,
    cache_lengths,
):
    tok_rows = layer_input.shape[0]
    seq_total = prompt_lengths.shape[0]
    same = (group_ids[:, None] == group_ids[None, :]).astype(jnp.float32)
    advantage = rewards - jnp.sum(same * rewards[None, :], axis=1) / GROUP
    first = lax.axis_index(("sec", "fsdp")) * tok_rows
    positions = first + jnp.arange(tok_rows, dtype=jnp.int32)
    seq_index = positions // SEQ_LEN
    offsets = positions % SEQ_LEN
    owner = seq_index[:, None] == jnp.arange(seq_total, dtype=jnp.int32)[None, :]
    prompt_tok = jnp.sum(jnp.where(owner, prompt_lengths[None, :], 0), axis=1)
    advantage_tok = jnp.sum(jnp.where(owner, advantage[None, :], jnp.float32(0.0)), axis=1)
    response = offsets >= prompt_tok
    token_weight = jnp.where(response, advantage_tok, jnp.float32(0.0))
    weighted = (value_cotangent.astype(jnp.float32) * token_weight[:, None]).astype(jnp.bfloat16)
    responses = lax.psum(jnp.sum(response.astype(jnp.float32)), ("sec", "fsdp"))
    transpose_contract = (((0,), (0,)), ((), ()))
    contract = (((1,), (1,)), ((), ()))
    steps_n = step_inputs.shape[0]
    rows_n = step_inputs.shape[1]
    width = step_inputs.shape[2]
    flat = step_inputs.reshape(steps_n * rows_n, width)
    columns = weighted
    input_grad = jnp.dot(
        columns,
        lax.all_gather(value_weight, ("sec", "fsdp"), axis=0, tiled=True),
        preferred_element_type=jnp.float32,
    ).astype(jnp.bfloat16)
    columns = weighted
    owned = lax.psum_scatter(
        lax.dot_general(
            columns, layer_input, transpose_contract, preferred_element_type=jnp.float32
        ),
        ("sec", "fsdp"),
        scatter_dimension=0,
        tiled=True,
    )
    new_shard = value_weight.astype(jnp.float32) - owned / responses
    widened = lax.all_gather(new_shard, "tp", axis=1, tiled=True)
    complete = lax.all_gather(widened, ("sec", "fsdp"), axis=0, tiled=True)
    span = complete.shape[0] // lax.axis_size("tp")
    head_rows = lax.dynamic_slice_in_dim(complete, lax.axis_index("tp") * span, span, 0)
    new_values = (
        lax.dot_general(
            flat.astype(jnp.float32),
            head_rows,
            contract,
            precision=lax.Precision.HIGHEST,
            preferred_element_type=jnp.float32,
        )
        .astype(jnp.bfloat16)
        .reshape(steps_n, rows_n, -1)
    )
    slots = cache_keys.shape[1]
    kv_local = key_weight.shape[0] // HEAD
    new_keys = (
        lax.dot_general(flat, key_weight, contract, preferred_element_type=jnp.float32)
        .astype(jnp.bfloat16)
        .reshape(steps_n, rows_n, -1)
    )
    query_five = queries.reshape(steps_n, rows_n, kv_local, QPK, HEAD)
    cache_k = cache_keys.reshape(rows_n, slots, kv_local, HEAD)
    cache_v = cache_values.reshape(rows_n, slots, kv_local, HEAD)
    fresh_k = new_keys.reshape(steps_n, rows_n, kv_local, HEAD)
    fresh_v = new_values.reshape(steps_n, rows_n, kv_local, HEAD)
    scale = 1.0 / HEAD**0.5
    cache_scores = (
        jnp.einsum("srkqd,rckd->srkqc", query_five, cache_k, preferred_element_type=jnp.float32)
        * scale
    )
    fresh_scores = (
        jnp.einsum("srkqd,trkd->srkqt", query_five, fresh_k, preferred_element_type=jnp.float32)
        * scale
    )
    live = (jnp.arange(slots, dtype=jnp.int32)[None, :] < cache_lengths[:, None])[
        None, :, None, None, :
    ]
    steps_idx = jnp.arange(steps_n, dtype=jnp.int32)
    causal = (steps_idx[None, :] <= steps_idx[:, None])[:, None, None, None, :]
    cache_scores = jnp.where(live, cache_scores, jnp.float32(-1e30))
    fresh_scores = jnp.where(causal, fresh_scores, jnp.float32(-1e30))
    top = jnp.maximum(
        jnp.max(cache_scores, axis=-1, keepdims=True), jnp.max(fresh_scores, axis=-1, keepdims=True)
    )
    cache_exp = jnp.where(live, jnp.exp(cache_scores - top), jnp.float32(0.0))
    fresh_exp = jnp.where(causal, jnp.exp(fresh_scores - top), jnp.float32(0.0))
    total = jnp.sum(cache_exp, axis=-1, keepdims=True) + jnp.sum(fresh_exp, axis=-1, keepdims=True)
    cache_prob = (cache_exp / total).astype(jnp.bfloat16)
    fresh_prob = (fresh_exp / total).astype(jnp.bfloat16)
    output = jnp.einsum(
        "srkqc,rckd->srkqd", cache_prob, cache_v, preferred_element_type=jnp.float32
    )
    output = output + jnp.einsum(
        "srkqt,trkd->srkqd", fresh_prob, fresh_v, preferred_element_type=jnp.float32
    )
    attended = output.astype(jnp.bfloat16).reshape(steps_n, rows_n, -1)
    return (input_grad, new_keys, new_values, attended)


def solution(mesh):
    in_specs = (
        P(("sec", "fsdp"), "tp"),
        P(("sec", "fsdp"), None),
        P(("sec", "fsdp"), "tp"),
        P(),
        P(),
        P(),
        P(None, ("sec", "fsdp"), None),
        P(None, ("sec", "fsdp"), "tp"),
        P("tp", None),
        P(("sec", "fsdp"), None, "tp"),
        P(("sec", "fsdp"), None, "tp"),
        P(("sec", "fsdp")),
    )
    out_specs = (
        P(("sec", "fsdp"), "tp"),
        P(None, ("sec", "fsdp"), "tp"),
        P(None, ("sec", "fsdp"), "tp"),
        P(None, ("sec", "fsdp"), "tp"),
    )
    return jax.shard_map(body, mesh=mesh, in_specs=in_specs, out_specs=out_specs, check_vma=False)
```

profile of v0, /device:TPU:1, one launch (start us, length us, event | category | flops | bytes accessed | tf_op | source)
XLA Modules:
  0.0 330.4 jit_solution(15209588842599914897)
XLA Ops:
  7.2 0.0 copy-start
  7.2 0.0 reduce-scatter.2.cloned.1.call-start
  7.3 1.0 select_reduce_fusion.1
  8.3 0.6 convert_reduce_fusion
  8.9 0.9 select_reduce_fusion.2
  9.8 0.7 multiply_subtract_fusion
  10.5 0.2 select_reduce_fusion
  10.8 12.1 %fusion = f32[1024,640]{1,0:T(8,128)} fusion(bf16[4096,640]{1,0:T(8,128)(2,1)} %param.12, bf16[4096,1024]{1,0:T(8,128)(2,1)} %param.13, f32[4096]{0:T(1024)S(1)} %broadcast_select_fusion), kind=kOutput, calls=%fused_computation.2 | convolution fusion | flops 5381292032 | bytes 16269312 | tf_op jit(solution)/shard_map/dot_general | solution.py:55
  22.9 0.0 reduce-scatter.2.cloned.1.call-update
  22.9 0.0 all-gather.6.cloned.1.call-start
  22.9 34.8 %psum.7 = f32[]{:T(128)} all-reduce(f32[]{:T(128)} %get-tuple-element.12), channel_id=1, replica_groups=mesh['sec'=4,'fsdp'=4,'tp'=8] {'sec','fsdp'}, use_global_device_ids=true, to_apply=%region_5.6 | all-reduce | flops 1 | bytes 8 | tf_op jit(solution)/shard_map/psum | solution.py:40
  57.7 40.4 %reduce-scatter.2.cloned.1.call-done = f32[64,640]{1,0:T(8,128)} async-done(((f32[1024,640]{1,0:T(8,128)}), f32[64,640]{1,0:T(8,128)}) %reduce-scatter.2.cloned.1.call-update) | async-done | bytes 163856 | tf_op jit(solution)/shard_map/reduce_scatter | solution.py:54
  98.2 2.3 divide_subtract_fusion
  100.4 0.0 all-gather.6.cloned.1.call-update
  100.5 0.0 all-gather.4.cloned.1.call-start
  100.5 0.7 all-gather.4.cloned.1.call-update
  101.2 0.0 all-gather.8.cloned.1.call-start
  101.2 34.4 %all-gather.6.cloned.1.call-done = f32[64,5120]{1,0:T(8,128)} async-done(((f32[64,640]{1,0:T(8,128)}), f32[64,5120]{1,0:T(8,128)}) %all-gather.6.cloned.1.call-update) | async-done | bytes 1310736 | tf_op jit(solution)/shard_map/all_gather | solution.py:63
  135.6 0.0 all-gather.8.cloned.1.call-update
  135.7 1.8 convolution_convert_fusion.1
  137.5 0.3 fusion.44
  137.8 0.1 iota_compare_fusion.1
  137.9 0.9 fusion.43
  138.8 0.1 fusion.26
  138.9 0.4 fusion.19
  139.3 2.1 fusion.9
  141.4 47.5 %all-gather.4.cloned.1.call-done = bf16[1024,640]{1,0:T(8,128)(2,1)} async-done(((bf16[64,640]{1,0:T(8,128)(2,1)}), bf16[1024,640]{1,0:T(8,128)(2,1)}) %all-gather.4.cloned.1.call-update) | async-done | bytes 1310736 | tf_op jit(solution)/shard_map/all_gather | solution.py:50
  188.9 11.1 %convolution_convert_fusion = bf16[4096,640]{1,0:T(8,128)(2,1)} fusion(bf16[1024,640]{1,0:T(8,128)(2,1)} %all-gather.4.cloned.1.call-done, bf16[4096,1024]{1,0:T(8,128)(2,1)} %param.13, f32[4096]{0:T(1024)S(1)} %broadcast_select_fusion), kind=kOutput, calls=%fused_computation.1 | convolution fusion | flops 5383913472 | bytes 14958592 | tf_op jit(solution)/shard_map/dot_general | solution.py:48
  200.0 119.9 %all-gather.8.cloned.1.call-done = f32[1024,5120]{1,0:T(8,128)} async-done(((f32[64,5120]{1,0:T(8,128)}), f32[1024,5120]{1,0:T(8,128)}) %all-gather.8.cloned.1.call-update) | async-done | bytes 20971536 | tf_op jit(solution)/shard_map/all_gather | solution.py:64
  319.9 3.0 fusion.15
  322.9 0.3 fusion.13
  323.2 0.6 copy.25
  (21 shorter events, 0.2 us)
Async XLA Ops:
  7.2 130.7 %copy-start = (bf16[4,2048,128]{2,1,0:T(8,128)(2,1)S(1)}, bf16[4,2048,128]{2,1,0:T(8,128)(2,1)}, u32[]{:S(2)}) copy-start(bf16[4,2048,128]{2,1,0:T(8,128)(2,1)} %param.21) | copy-start | bytes 6291460
  7.2 91.0 %reduce-scatter.2.cloned.1.call-start = ((), (), s32[]{:S(2)}) async-start(), calls=%async_computation.2 | async-start | bytes 2785280 | tf_op jit(solution)/shard_map/reduce_scatter | solution.py:54
  10.7 87.4 %copy-start.1 = (bf16[64,640]{1,0:T(8,128)(2,1)S(1)}, bf16[64,640]{1,0:T(8,128)(2,1)}, u32[]{:S(2)}) copy-start(bf16[64,640]{1,0:T(8,128)(2,1)} %param.14) | copy-start | bytes 245764
  10.8 124.9 %copy-start.2 = (bf16[4,4,5120]{2,1,0:T(4,128)(2,1)S(1)}, bf16[4,4,5120]{2,1,0:T(4,128)(2,1)}, u32[]{:S(2)}) copy-start(bf16[4,4,5120]{2,1,0:T(4,128)(2,1)} %param.18) | copy-start | bytes 491524
  10.8 124.9 %copy-start.3 = (bf16[4,4,1024]{2,1,0:T(4,128)(2,1)S(1)}, bf16[4,4,1024]{2,1,0:T(4,128)(2,1)}, u32[]{:S(2)}) copy-start(bf16[4,4,1024]{2,1,0:T(4,128)(2,1)} %param.19) | copy-start | bytes 98308
  22.8 114.9 %copy-start.6 = (s32[4]{0:T(128)S(1)}, s32[4]{0:T(128)}, u32[]{:S(2)}) copy-start(s32[4]{0:T(128)} %param.23) | copy-start | bytes 52
  22.9 112.7 %all-gather.6.cloned.1.call-start = ((), (), s32[]{:S(2)}) async-start(), calls=%async_computation.3 | async-start | bytes 1474560 | tf_op jit(solution)/shard_map/all_gather | solution.py:63
  100.5 88.5 %all-gather.4.cloned.1.call-start = ((), (), s32[]{:S(2)}) async-start(), calls=%async_computation.1 | async-start | bytes 1392640 | tf_op jit(solution)/shard_map/all_gather | solution.py:50
  101.2 218.7 %all-gather.8.cloned.1.call-start = ((), (), s32[]{:S(2)}) async-start(), calls=%async_computation.4 | async-start | bytes 22282240 | tf_op jit(solution)/shard_map/all_gather | solution.py:64
  137.5 3.9 %copy-start.4 = (bf16[16,128]{1,0:T(8,128)(2,1)}, bf16[16,128]{1,0:T(8,128)(2,1)S(1)}, u32[]{:S(2)}) copy-start(bf16[16,128]{1,0:T(8,128)(2,1)S(1)} %convolution_convert_fusion.1) | copy-start | bytes 12292
  322.9 0.9 copy-start.5
Sparse Core Ops, SparseCore 0:
  23.0 75.1 reduce-scatter.1
  100.6 34.9 all-gather.5
  138.3 50.5 all-gather.3
  191.5 128.3 all-gather.7
where the time goes:
time: 331 us; the launch traced here: 330 us
  waiting for transfers between devices  243 us (73%)
  blocking collectives  34.8 us (11%)
  matrix products  31.5 us (10%)
  between operations  13.9 us (4%)
  other arithmetic  6.3 us (2%)
    all_gather x1, waiting for transfers between devices, body(): complete = lax.all_gather(widened, ('sec', 'fsdp'), axis=0, tiled=True)  120 us
    all_gather x1, waiting for transfers between devices, body(): lax.all_gather(value_weight, ('sec', 'fsdp'), axis=0, tiled=True)  47.5 us
    reduce_scatter x1, waiting for transfers between devices, body(): lax.psum_scatter(lax.dot_general(columns, layer_input, transpose_contract...  40.4 us
    psum x1, blocking collectives, body(): responses = lax.psum(jnp.sum(response.astype(jnp.float32)), ('sec', 'fsdp'))  34.8 us
    all_gather x1, waiting for transfers between devices, body(): widened = lax.all_gather(new_shard, 'tp', axis=1, tiled=True)  34.4 us
    dot_general x1, matrix products, body(): lax.dot_general(columns, layer_input, transpose_contract, preferred_eleme...  12.1 us
    dot_general x1, matrix products, body(): jnp.dot(columns, lax.all_gather(value_weight, ('sec', 'fsdp'), axis=0, ti...  11.1 us
  transfers between devices with their start and end apart: 4, of which 4 were waited for; matrix products, arithmetic and copies ran while one was open for 5% of the time, Pallas kernels for 0%

commit v1 on v0

v1 whole, which is shorter than its diff:
```python
import functools

import jax
import jax.numpy as jnp
from jax import lax
from jax.experimental import pallas as pl
from jax.experimental.pallas import tpu as pltpu
from jax.sharding import PartitionSpec as P

HEAD = 128
QPK = 8
SEQ_LEN = 1024
GROUP = 8
SKIP = 128
LIVE = SEQ_LEN - SKIP
MESH = pl.DeviceIdType.MESH
F32 = jnp.float32
BF16 = jnp.bfloat16
NT = (((1,), (1,)), ((), ()))
NN = (((1,), (0,)), ((), ()))


def flip(value, bits):
    for at in range(3):
        unit = 1 << at
        if bits & unit:
            value = value + unit - 2 * unit * lax.rem(lax.div(value, unit), 2)
    return value


def dot(a, b, dims):
    return lax.dot_general(a, b, dims, preferred_element_type=F32)


def kernel(
    layer_ref,
    cot_ref,
    vw_ref,
    rewards_ref,
    groups_ref,
    prompts_ref,
    step_ref,
    query_ref,
    kw_ref,
    ck_ref,
    cv_ref,
    len_ref,
    grad_ref,
    nk_ref,
    nv_ref,
    att_ref,
    layer_v,
    cot_v,
    vw_v,
    step_v,
    query_v,
    kw_v,
    ck_v,
    cv_v,
    flat_v,
    xall_v,
    wall_v,
    a_v,
    away_v,
    home_v,
    core_v,
    recv_v,
    out_v,
    zero_v,
    att_v,
    load_sem,
    out_sem,
    zero_sem,
    x_send,
    x_recv,
    w_send,
    w_recv,
    pair_send,
    pair_recv,
    core_send,
    core_recv,
    rs_send,
    rs_recv,
    ready_sem,
):
    sec = lax.axis_index("sec")
    fs = lax.axis_index("fsdp")
    tp = lax.axis_index("tp")
    core = lax.rem(fs, 2)
    group = sec * 4 + fs
    seqs = layer_ref.shape[0] // SEQ_LEN
    n_seq = rewards_ref.shape[0]
    cols = layer_ref.shape[1]

    def device(q, dc, dt):
        return (flip(sec, q // 2), flip(fs, (q % 2) * 2 + dc), flip(tp, dt))

    barrier = pltpu.get_barrier_semaphore()
    for q in range(8):
        for dc in range(2):
            if q or dc:
                pl.semaphore_signal(barrier, inc=1, device_id=device(q, dc, 0), device_id_type=MESH)
    for dt in range(1, 8):
        pl.semaphore_signal(barrier, inc=1, device_id=device(0, 0, dt), device_id_type=MESH)

    def load(src, dst, at):
        copy = pltpu.make_async_copy(src, dst, load_sem.at[at])
        copy.start()
        return copy

    step_load = load(step_ref, step_v, 0)
    vw_load = load(vw_ref, vw_v, 1)
    query_load = load(query_ref, query_v, 2)
    kw_load = load(kw_ref, kw_v, 3)
    rows_n = ck_ref.shape[0]
    ck_loads = [load(ck_ref.at[r], ck_v.at[r], 4 + r) for r in range(rows_n)]
    cv_loads = [load(cv_ref.at[r], cv_v.at[r], 8 + r) for r in range(rows_n)]
    cot_loads = [
        load(cot_ref.at[pl.ds(s * SEQ_LEN + SKIP, LIVE)], cot_v.at[pl.ds(s * LIVE, LIVE)], 12 + s)
        for s in range(seqs)
    ]
    layer_loads = [
        load(layer_ref.at[pl.ds(s * SEQ_LEN + SKIP, LIVE)], layer_v.at[pl.ds(s * LIVE, LIVE)], 16 + s)
        for s in range(seqs)
    ]

    zero_v[...] = jnp.zeros_like(zero_v)
    zero_copies = [
        pltpu.make_async_copy(zero_v, grad_ref.at[pl.ds(s * SEQ_LEN, SKIP)], zero_sem.at[s])
        for s in range(seqs)
    ]
    for copy in zero_copies:
        copy.start()

    first = group * seqs
    own_groups = [groups_ref[first + s] for s in range(seqs)]
    own_prompts = [prompts_ref[first + s] for s in range(seqs)]

    def scan(j, carry):
        prompts = carry[0] + prompts_ref[j]
        reward = rewards_ref[j]
        sums = [
            c + jnp.where(groups_ref[j] == g, reward, F32(0.0))
            for c, g in zip(carry[1:], own_groups)
        ]
        return (prompts, *sums)

    scanned = lax.fori_loop(0, n_seq, scan, (jnp.int32(0),) + (F32(0.0),) * seqs)
    responses = (n_seq * SEQ_LEN - scanned[0]).astype(F32)
    advantage = [rewards_ref[first + s] - scanned[1 + s] / F32(GROUP) for s in range(seqs)]

    step_load.wait()
    flat_v[...] = jnp.concatenate(
        [step_v[s].astype(F32) for s in range(step_v.shape[0])], axis=0
    ).astype(BF16)
    own_x = flat_v.at[:, pl.ds(pl.multiple_of(tp * cols, 128), cols)]
    xall_v[0] = flat_v[:, pl.ds(pl.multiple_of(tp * cols, 128), cols)]
    vw_load.wait()
    wall_v[sec * 2 + lax.div(fs, 2), core] = vw_v[...]

    pl.semaphore_wait(barrier, 22)
    for dt in range(1, 8):
        pl.semaphore_signal(ready_sem, inc=1, device_id=device(0, 0, dt), device_id_type=MESH)
    for dc in (0, 1):
        for q in range(8):
            if q or dc:
                pltpu.make_async_remote_copy(
                    src_ref=own_x,
                    dst_ref=xall_v.at[dc * 8 + q],
                    send_sem=x_send,
                    recv_sem=x_recv,
                    device_id=device(q, dc, 0),
                    device_id_type=MESH,
                ).start()
    for q in range(1, 8):
        pltpu.make_async_remote_copy(
            src_ref=vw_v,
            dst_ref=wall_v.at[sec * 2 + lax.div(fs, 2), core],
            send_sem=w_send,
            recv_sem=w_recv,
            device_id=device(q, 0, 0),
            device_id_type=MESH,
        ).start()

    kw_load.wait()
    new_keys = dot(flat_v[...], kw_v[...], NT).astype(BF16)
    nk_ref[...] = new_keys

    query_load.wait()
    steps_n = query_v.shape[0]
    q16 = jnp.concatenate([query_v[s].astype(F32) for s in range(steps_n)], axis=0).astype(BF16)
    stacked = jnp.concatenate([q16[:, h * HEAD : (h + 1) * HEAD] for h in range(QPK)], axis=0)
    n_q = QPK * steps_n * rows_n
    to_r = lax.broadcasted_iota(jnp.int32, (n_q, n_q), 0)
    frm = lax.broadcasted_iota(jnp.int32, (n_q, n_q), 1)
    per = steps_n * QPK
    src_of = lax.rem(to_r, QPK) * 16 + lax.rem(lax.div(to_r, QPK), steps_n) * rows_n + lax.div(to_r, per)
    perm = (frm == src_of).astype(F32).astype(BF16)
    scale = F32(1.0 / HEAD**0.5)
    queries = dot(perm, stacked, NN).astype(BF16)
    fresh = dot(queries, new_keys, NT) * scale
    i_at = lax.broadcasted_iota(jnp.int32, fresh.shape, 0)
    j_at = lax.broadcasted_iota(jnp.int32, fresh.shape, 1)
    causal = (lax.div(i_at, per) == lax.rem(j_at, rows_n)) & (
        lax.div(j_at, rows_n) <= lax.rem(lax.div(i_at, QPK), steps_n)
    )
    fresh = jnp.where(causal, fresh, F32(-1e30))
    fresh_top = jnp.max(fresh, axis=1, keepdims=True)
    slots = ck_v.shape[1]
    slot_at = lax.broadcasted_iota(jnp.int32, (per, slots), 1)
    fresh_probs = []
    for r in range(rows_n):
        part = slice(r * per, (r + 1) * per)
        ck_loads[r].wait()
        scores = dot(queries[part], ck_v[r], NT) * scale
        live = slot_at < len_ref[r]
        scores = jnp.where(live, scores, F32(-1e30))
        top = jnp.maximum(jnp.max(scores, axis=1, keepdims=True), fresh_top[part])
        e = jnp.where(live, jnp.exp(scores - top), F32(0.0))
        fe = jnp.where(causal[part], jnp.exp(fresh[part] - top), F32(0.0))
        total = jnp.sum(e, axis=1, keepdims=True) + jnp.sum(fe, axis=1, keepdims=True)
        inv = F32(1.0) / total
        cv_loads[r].wait()
        att_v[part, :] = dot((e * inv).astype(BF16), cv_v[r], NN)
        fresh_probs.append((fe * inv).astype(BF16).astype(F32))
    fresh_prob = jnp.concatenate(fresh_probs, axis=0).astype(BF16)

    rows_at = lax.broadcasted_iota(jnp.int32, (128, 128), 0)
    wide = cot_v.shape[1]
    for s in range(seqs):
        cot_loads[s].wait()

        def weigh(j, _, s=s):
            at = pl.multiple_of(s * LIVE + j * 128, 128)
            weight = jnp.where(rows_at + (SKIP + j * 128) >= own_prompts[s], advantage[s], F32(0.0))
            for n in range(wide // 128):
                span = slice(n * 128, (n + 1) * 128)
                cot_v[pl.ds(at, 128), span] = (cot_v[pl.ds(at, 128), span].astype(F32) * weight).astype(BF16)
            return 0

        lax.fori_loop(0, LIVE // 128, weigh, 0)

    pltpu.make_async_copy(xall_v.at[pl.ds(1, 15)], xall_v.at[pl.ds(1, 15)], x_recv).wait()
    x_all = xall_v[...].reshape(256, cols)
    for copy in layer_loads:
        copy.wait()
    tokens = layer_v.shape[0]
    blk = 512

    def outer(j, _):
        at = pl.multiple_of(j * blk, blk)
        a_v[:, pl.ds(at, blk)] = dot(xall_v[...].reshape(256, cols), layer_v[pl.ds(at, blk), :], NT).astype(BF16)
        return 0

    lax.fori_loop(0, tokens // blk, outer, 0)

    pltpu.make_async_copy(wall_v.at[pl.ds(0, 7), 0], wall_v.at[pl.ds(0, 7), 0], w_recv).wait()
    pair = pltpu.make_async_remote_copy(
        src_ref=wall_v.at[:, core],
        dst_ref=wall_v.at[:, core],
        send_sem=pair_send,
        recv_sem=pair_recv,
        device_id=device(0, 1, 0),
        device_id_type=MESH,
    )
    pair.start()

    inv_resp = F32(1.0) / responses
    own = dot(x_all, jnp.concatenate([vw_v[...]] * 4, axis=0), NT)
    quarter = lax.div(lax.broadcasted_iota(jnp.int32, (256, 256), 1), 64)
    own = jnp.where(quarter == lax.rem(group, 4), own, F32(0.0))
    own_chunk = lax.div(group, 4)
    tp_hi, tp_lo = lax.div(tp, 2), lax.rem(tp, 2)
    copies = []
    for k in range(4):
        at = flip(tp_hi, k)
        weighted = cot_v[:, pl.ds(pl.multiple_of(at * 256, 256), 256)]
        part = jnp.where(own_chunk == at, own, F32(0.0)) - dot(a_v[...], weighted, NN) * inv_resp
        for j in range(2):
            home_v[k, j] = part[:128, j * 128 : (j + 1) * 128]
            away_v[k, j] = part[128:, j * 128 : (j + 1) * 128]
        copy = pltpu.make_async_remote_copy(
            src_ref=away_v.at[k],
            dst_ref=core_v.at[k],
            send_sem=core_send.at[k],
            recv_sem=core_recv.at[k],
            device_id=device(0, 1, 0),
            device_id_type=MESH,
        )
        copy.start()
        copies.append(copy)
    pl.semaphore_wait(ready_sem, 7)

    def scatter(k):
        copies[k].wait_recv()
        home_v[k] = home_v[k] + core_v[k]
        for e in range(2):
            j = flip(tp_lo, e)
            dt = 2 * k + e
            for q in range(8):
                if q or dt:
                    pltpu.make_async_remote_copy(
                        src_ref=home_v.at[k, j, pl.ds(q * 16, 16)],
                        dst_ref=recv_v.at[q * 8 + dt],
                        send_sem=rs_send,
                        recv_sem=rs_recv,
                        device_id=device(q, 0, dt),
                        device_id_type=MESH,
                    ).start()
        if k == 0:
            recv_v[0] = home_v[0, tp_lo, 0:16, :]

    for k in range(4):
        scatter(k)

    pair.wait()
    half = LIVE // 2

    def grad(j, _):
        at = pl.multiple_of(j * half, half)
        out_v[pl.ds(at, half), :] = dot(
            cot_v[pl.ds(at, half), :], wall_v[...].reshape(wide, cols), NN
        ).astype(BF16)
        to = lax.div(j, 2) * SEQ_LEN + SKIP + lax.rem(j, 2) * half
        pltpu.make_async_copy(
            out_v.at[pl.ds(at, half)], grad_ref.at[pl.ds(pl.multiple_of(to, 64), half)], out_sem
        ).start()
        return 0

    lax.fori_loop(0, tokens // half, grad, 0)

    pltpu.make_async_copy(recv_v.at[pl.ds(1, 63)], recv_v.at[pl.ds(1, 63)], rs_recv).wait()
    new_values = jnp.sum(recv_v[...], axis=0).astype(BF16)
    nv_ref[...] = new_values
    done = (att_v[...] + dot(fresh_prob, new_values, NN)).astype(BF16)
    back = dot(perm, done, (((0,), (0,)), ((), ()))).astype(BF16)
    for h in range(QPK):
        att_ref[:, h * HEAD : (h + 1) * HEAD] = back[h * 16 : (h + 1) * 16]

    pltpu.make_async_copy(recv_v.at[pl.ds(1, 63)], recv_v.at[pl.ds(1, 63)], rs_send).wait()
    pltpu.make_async_copy(xall_v.at[pl.ds(1, 15)], xall_v.at[pl.ds(1, 15)], x_send).wait()
    pltpu.make_async_copy(wall_v.at[pl.ds(0, 7), 0], wall_v.at[pl.ds(0, 7), 0], w_send).wait()
    for copy in copies:
        copy.wait_send()
    for copy in zero_copies:
        copy.wait()
    pltpu.make_async_copy(out_v, out_v, out_sem).wait()


def body(*args):
    layer, cot, vw, rewards, groups, prompts, step, query, kw, ck, cv, lengths = args
    steps_n, rows_n, width = step.shape
    n = steps_n * rows_n
    seqs = layer.shape[0] // SEQ_LEN
    tokens = seqs * LIVE
    cols = layer.shape[1]
    hbm = pl.BlockSpec(memory_space=pl.ANY)
    smem = pl.BlockSpec(memory_space=pltpu.SMEM)
    vmem = pl.BlockSpec(memory_space=pltpu.VMEM)
    dma = pltpu.SemaphoreType.DMA
    grad, new_keys, new_values, attended = pl.pallas_call(
        kernel,
        out_shape=(
            jax.ShapeDtypeStruct(layer.shape, BF16),
            jax.ShapeDtypeStruct((n, HEAD), BF16),
            jax.ShapeDtypeStruct((n, HEAD), BF16),
            jax.ShapeDtypeStruct((n, QPK * HEAD), BF16),
        ),
        in_specs=[hbm, hbm, hbm, smem, smem, smem, hbm, hbm, hbm, hbm, hbm, smem],
        out_specs=(hbm, vmem, vmem, vmem),
        scratch_shapes=[
            pltpu.VMEM((tokens, cols), BF16),
            pltpu.VMEM((tokens, cot.shape[1]), BF16),
            pltpu.VMEM(vw.shape, BF16),
            pltpu.VMEM(step.shape, BF16),
            pltpu.VMEM(query.shape, BF16),
            pltpu.VMEM(kw.shape, BF16),
            pltpu.VMEM(ck.shape, BF16),
            pltpu.VMEM(cv.shape, BF16),
            pltpu.VMEM((n, width), BF16),
            pltpu.VMEM((16, n, cols), BF16),
            pltpu.VMEM((8, 2, *vw.shape), BF16),
            pltpu.VMEM((256, tokens), BF16),
            pltpu.VMEM((4, 2, 128, 128), F32),
            pltpu.VMEM((4, 2, 128, 128), F32),
            pltpu.VMEM((4, 2, 128, 128), F32),
            pltpu.VMEM((64, n, HEAD), F32),
            pltpu.VMEM((tokens, cols), BF16),
            pltpu.VMEM((SKIP, cols), BF16),
            pltpu.VMEM((128, HEAD), F32),
            dma((20,)),
            dma,
            dma((4,)),
            dma,
            dma,
            dma,
            dma,
            dma,
            dma,
            dma((4,)),
            dma((4,)),
            dma,
            dma,
            pltpu.SemaphoreType.REGULAR,
        ],
        compiler_params=pltpu.CompilerParams(
            collective_id=0, has_side_effects=True, vmem_limit_bytes=56 * 1024 * 1024
        ),
    )(*args)
    return (
        grad,
        new_keys.reshape(steps_n, rows_n, HEAD),
        new_values.reshape(steps_n, rows_n, HEAD),
        attended.reshape(steps_n, rows_n, QPK * HEAD),
    )


def solution(mesh):
    tokens = ("sec", "fsdp")
    in_specs = (
        P(tokens, "tp"),
        P(tokens, None),
        P(tokens, "tp"),
        P(),
        P(),
        P(),
        P(None, tokens, None),
        P(None, tokens, "tp"),
        P("tp", None),
        P(tokens, None, "tp"),
        P(tokens, None, "tp"),
        P(tokens),
    )
    out_specs = (
        P(tokens, "tp"),
        P(None, tokens, "tp"),
        P(None, tokens, "tp"),
        P(None, tokens, "tp"),
    )
    return jax.shard_map(body, mesh=mesh, in_specs=in_specs, out_specs=out_specs, check_vma=False)
```

time: 331 us -> 48.4 us (0.15)
  waiting for transfers between devices: 243 us -> 0 us
  Pallas kernels: 0 us -> 39.3 us
  blocking collectives: 34.8 us -> 0 us
  matrix products: 31.5 us -> 0 us
  between operations: 13.9 us -> 0.65 us
  local copies, waits for them, and re-layouts: 0.75 us -> 7.88 us
  other arithmetic: 6.3 us -> 0 us
    all_gather x3 -> x0, waiting for transfers between devices: 202 us -> none  [the longest x1 120 us: body(): complete = lax.all_gather(widened, ('sec', 'fsdp'), axis=0, tiled=True)]
    reduce_scatter x1 -> x0, waiting for transfers between devices: 40.4 us -> none  [body(): lax.psum_scatter(lax.dot_general(columns, layer_input, transpose_contract...]
    pallas_call x0 -> x1, Pallas kernels: none -> 39.3 us  [body(): pl.pallas_call(kernel, out_shape=(jax.ShapeDtypeStruct(layer.shape, BF16)...]
    psum x1 -> x0, blocking collectives: 34.8 us -> none  [body(): responses = lax.psum(jnp.sum(response.astype(jnp.float32)), ('sec', 'fsdp'))]
    dot_general x8 -> x0, matrix products: 31.5 us -> none  [the longest x1 12.1 us: body(): lax.dot_general(columns, layer_input, transpose_contract, preferred_eleme...]
    unnamed x15 -> x7, local copies, waits for them, and re-layouts: 0.67 us -> 6.49 us
  transfers between devices with their start and end apart: 4 -> 0, of which waited for: 4 -> 0; matrix products, arithmetic and copies ran while one was open for 5% -> 0% of each run, Pallas kernels for 0% -> 0%
where the time goes in v1:
time: 48.4 us; the launch traced here: 47.9 us
  Pallas kernels  39.3 us (81%)
  local copies, waits for them, and re-layouts  7.88 us (16%)
  between operations  0.65 us (1%)
    pallas_call x1, Pallas kernels, body(): pl.pallas_call(kernel, out_shape=(jax.ShapeDtypeStruct(layer.shape, BF16)...  39.3 us
    unnamed x7, local copies, waits for them, and re-layouts  6.49 us
    reshape x1, local copies, waits for them, and re-layouts, body(): attended.reshape(steps_n, rows_n, QPK * HEAD)  1.39 us

profile of v1, /device:TPU:1, one launch (start us, length us, event | category | flops | bytes accessed | tf_op | source)
XLA Modules:
  0.0 47.9 jit_solution(16288683451357009263)
XLA Ops:
  0.6 39.3 %shard_map.147 = (bf16[4096,640]{1,0:T(8,128)(2,1)}, bf16[16,128]{1,0:T(8,128)(2,1)}, bf16[16,128]{1,0:T(8,128)(2,1)}, bf16[16,1024]{1,0:T(8,128)(2,1)}) custom-call(bf16[4096,640]{1,0:T(8,128)(2,1)} %layer_ref.1, bf16[4096,1024]{1,0:T(8,128)(2,1)} %cot_ref.1, bf16[64,640]{1,0:T(8,128)(2,1)} %vw_ref.1, f32[64]{0:T(128)} %rewards_ref.1, s32[64]{0:T(128)} %groups_ref.1, ...), custom_call_target="tpu_custom_call" | custom-call | tf_op jit(solution)/shard_map/pallas_call | solution.py:361
  40.0 1.4 %reshape.19 = bf16[4,4,1024]{2,1,0:T(4,128)(2,1)} reshape(bf16[16,1024]{1,0:T(8,128)(2,1)} %get-tuple-element.11) | data formatting | bytes 65536 | tf_op jit(solution)/shard_map/reshape | solution.py:414
  41.4 0.0 copy-start.1
  41.4 0.0 copy-start
  41.4 5.3 %copy.19 = bf16[4096,640]{1,0:T(8,128)(2,1)} copy(bf16[4096,640]{1,0:T(8,128)(2,1)} %get-tuple-element.16) | data formatting | bytes 10485760
  46.7 0.0 copy-done.1
  46.7 0.6 %copy.20 = bf16[4,4,128]{2,1,0:T(4,128)(2,1)} copy(bf16[4,4,128]{2,1,0:T(4,128)(2,1)S(1)} %bitcast.3) | data formatting | bytes 8192
  47.3 0.0 copy-done
  47.3 0.6 %copy.21 = bf16[4,4,128]{2,1,0:T(4,128)(2,1)} copy(bf16[4,4,128]{2,1,0:T(4,128)(2,1)S(1)} %bitcast.2) | data formatting | bytes 8192
Async XLA Ops:
  41.4 5.3 %copy-start.1 = (bf16[16,128]{1,0:T(8,128)(2,1)S(1)}, bf16[16,128]{1,0:T(8,128)(2,1)}, u32[]{:S(2)}) copy-start(bf16[16,128]{1,0:T(8,128)(2,1)} %get-tuple-element.9) | copy-start | bytes 12292
  41.4 5.9 %copy-start = (bf16[16,128]{1,0:T(8,128)(2,1)S(1)}, bf16[16,128]{1,0:T(8,128)(2,1)}, u32[]{:S(2)}) copy-start(bf16[16,128]{1,0:T(8,128)(2,1)} %get-tuple-element.10) | copy-start | bytes 12292

commit v2 on v1

--- a/solution.py
+++ b/solution.py
@@ -65,14 +65,12 @@
     home_v,
     core_v,
     recv_v,
-    out_v,
-    zero_v,
     att_v,
     load_sem,
-    out_sem,
-    zero_sem,
     x_send,
     x_recv,
+    xp_send,
+    xp_recv,
     w_send,
     w_recv,
     pair_send,
@@ -95,11 +93,13 @@
     def device(q, dc, dt):
         return (flip(sec, q // 2), flip(fs, (q % 2) * 2 + dc), flip(tp, dt))
 
+    def near(q):
+        return 4 * (q % 2)
+
     barrier = pltpu.get_barrier_semaphore()
-    for q in range(8):
-        for dc in range(2):
-            if q or dc:
-                pl.semaphore_signal(barrier, inc=1, device_id=device(q, dc, 0), device_id_type=MESH)
+    for q in (4, 5, 2, 3, 6, 7, 1):
+        pl.semaphore_signal(barrier, inc=1, device_id=device(q, 0, near(q)), device_id_type=MESH)
+    pl.semaphore_signal(barrier, inc=1, device_id=device(0, 1, 0), device_id_type=MESH)
     for dt in range(1, 8):
         pl.semaphore_signal(barrier, inc=1, device_id=device(0, 0, dt), device_id_type=MESH)
 
@@ -124,14 +124,6 @@
         for s in range(seqs)
     ]
 
-    zero_v[...] = jnp.zeros_like(zero_v)
-    zero_copies = [
-        pltpu.make_async_copy(zero_v, grad_ref.at[pl.ds(s * SEQ_LEN, SKIP)], zero_sem.at[s])
-        for s in range(seqs)
-    ]
-    for copy in zero_copies:
-        copy.start()
-
     first = group * seqs
     own_groups = [groups_ref[first + s] for s in range(seqs)]
     own_prompts = [prompts_ref[first + s] for s in range(seqs)]
@@ -153,38 +145,41 @@
     flat_v[...] = jnp.concatenate(
         [step_v[s].astype(F32) for s in range(step_v.shape[0])], axis=0
     ).astype(BF16)
-    own_x = flat_v.at[:, pl.ds(pl.multiple_of(tp * cols, 128), cols)]
     xall_v[0] = flat_v[:, pl.ds(pl.multiple_of(tp * cols, 128), cols)]
     vw_load.wait()
-    wall_v[sec * 2 + lax.div(fs, 2), core] = vw_v[...]
-
-    pl.semaphore_wait(barrier, 22)
+    row_at = sec * 2 + lax.div(fs, 2)
+    wall_v[row_at, core] = vw_v[...]
+
+    kw_load.wait()
+    new_keys = dot(flat_v[...], kw_v[...], NT).astype(BF16)
+    nk_ref[...] = new_keys
+
+    pl.semaphore_wait(barrier, 15)
+    for q in (4, 5, 2, 3, 6, 7, 1):
+        at = pl.multiple_of(flip(tp, near(q)) * cols, 128)
+        pltpu.make_async_remote_copy(
+            src_ref=flat_v.at[:, pl.ds(at, cols)],
+            dst_ref=xall_v.at[q],
+            send_sem=x_send,
+            recv_sem=x_recv,
+            device_id=device(q, 0, near(q)),
+            device_id_type=MESH,
+        ).start()
     for dt in range(1, 8):
         pl.semaphore_signal(ready_sem, inc=1, device_id=device(0, 0, dt), device_id_type=MESH)
-    for dc in (0, 1):
-        for q in range(8):
-            if q or dc:
-                pltpu.make_async_remote_copy(
-                    src_ref=own_x,
-                    dst_ref=xall_v.at[dc * 8 + q],
-                    send_sem=x_send,
-                    recv_sem=x_recv,
-                    device_id=device(q, dc, 0),
-                    device_id_type=MESH,
-                ).start()
-    for q in range(1, 8):
+
+    def send_weight(q):
         pltpu.make_async_remote_copy(
             src_ref=vw_v,
-            dst_ref=wall_v.at[sec * 2 + lax.div(fs, 2), core],
+            dst_ref=wall_v.at[row_at, core],
             send_sem=w_send,
             recv_sem=w_recv,
             device_id=device(q, 0, 0),
             device_id_type=MESH,
         ).start()
 
-    kw_load.wait()
-    new_keys = dot(flat_v[...], kw_v[...], NT).astype(BF16)
-    nk_ref[...] = new_keys
+    for q in (4, 2, 6):
+        send_weight(q)
 
     query_load.wait()
     steps_n = query_v.shape[0]
@@ -225,10 +220,25 @@
         fresh_probs.append((fe * inv).astype(BF16).astype(F32))
     fresh_prob = jnp.concatenate(fresh_probs, axis=0).astype(BF16)
 
+    pl.semaphore_wait(ready_sem, 7)
+    for q in (5, 3, 7, 1):
+        send_weight(q)
+
     rows_at = lax.broadcasted_iota(jnp.int32, (128, 128), 0)
     wide = cot_v.shape[1]
     for s in range(seqs):
         cot_loads[s].wait()
+        if s == seqs - 1:
+            pltpu.make_async_copy(xall_v.at[pl.ds(1, 7)], xall_v.at[pl.ds(1, 7)], x_recv).wait()
+            x_pair = pltpu.make_async_remote_copy(
+                src_ref=xall_v.at[pl.ds(0, 8)],
+                dst_ref=xall_v.at[pl.ds(8, 8)],
+                send_sem=xp_send,
+                recv_sem=xp_recv,
+                device_id=device(0, 1, 0),
+                device_id_type=MESH,
+            )
+            x_pair.start()
 
         def weigh(j, _, s=s):
             at = pl.multiple_of(s * LIVE + j * 128, 128)
@@ -240,7 +250,7 @@
 
         lax.fori_loop(0, LIVE // 128, weigh, 0)
 
-    pltpu.make_async_copy(xall_v.at[pl.ds(1, 15)], xall_v.at[pl.ds(1, 15)], x_recv).wait()
+    x_pair.wait_recv()
     x_all = xall_v[...].reshape(256, cols)
     for copy in layer_loads:
         copy.wait()
@@ -253,17 +263,6 @@
         return 0
 
     lax.fori_loop(0, tokens // blk, outer, 0)
-
-    pltpu.make_async_copy(wall_v.at[pl.ds(0, 7), 0], wall_v.at[pl.ds(0, 7), 0], w_recv).wait()
-    pair = pltpu.make_async_remote_copy(
-        src_ref=wall_v.at[:, core],
-        dst_ref=wall_v.at[:, core],
-        send_sem=pair_send,
-        recv_sem=pair_recv,
-        device_id=device(0, 1, 0),
-        device_id_type=MESH,
-    )
-    pair.start()
 
     inv_resp = F32(1.0) / responses
     own = dot(x_all, jnp.concatenate([vw_v[...]] * 4, axis=0), NT)
@@ -272,24 +271,6 @@
     own_chunk = lax.div(group, 4)
     tp_hi, tp_lo = lax.div(tp, 2), lax.rem(tp, 2)
     copies = []
-    for k in range(4):
-        at = flip(tp_hi, k)
-        weighted = cot_v[:, pl.ds(pl.multiple_of(at * 256, 256), 256)]
-        part = jnp.where(own_chunk == at, own, F32(0.0)) - dot(a_v[...], weighted, NN) * inv_resp
-        for j in range(2):
-            home_v[k, j] = part[:128, j * 128 : (j + 1) * 128]
-            away_v[k, j] = part[128:, j * 128 : (j + 1) * 128]
-        copy = pltpu.make_async_remote_copy(
-            src_ref=away_v.at[k],
-            dst_ref=core_v.at[k],
-            send_sem=core_send.at[k],
-            recv_sem=core_recv.at[k],
-            device_id=device(0, 1, 0),
-            device_id_type=MESH,
-        )
-        copy.start()
-        copies.append(copy)
-    pl.semaphore_wait(ready_sem, 7)
 
     def scatter(k):
         copies[k].wait_recv()
@@ -311,20 +292,45 @@
             recv_v[0] = home_v[0, tp_lo, 0:16, :]
 
     for k in range(4):
-        scatter(k)
+        at = flip(tp_hi, k)
+        weighted = cot_v[:, pl.ds(pl.multiple_of(at * 256, 256), 256)]
+        part = jnp.where(own_chunk == at, own, F32(0.0)) - dot(a_v[...], weighted, NN) * inv_resp
+        for j in range(2):
+            home_v[k, j] = part[:128, j * 128 : (j + 1) * 128]
+            away_v[k, j] = part[128:, j * 128 : (j + 1) * 128]
+        copy = pltpu.make_async_remote_copy(
+            src_ref=away_v.at[k],
+            dst_ref=core_v.at[k],
+            send_sem=core_send.at[k],
+            recv_sem=core_recv.at[k],
+            device_id=device(0, 1, 0),
+            device_id_type=MESH,
+        )
+        copy.start()
+        copies.append(copy)
+        if k:
+            scatter(k - 1)
+    scatter(3)
+
+    pltpu.make_async_copy(wall_v.at[pl.ds(0, 7), 0], wall_v.at[pl.ds(0, 7), 0], w_recv).wait()
+    pair = pltpu.make_async_remote_copy(
+        src_ref=wall_v.at[:, core],
+        dst_ref=wall_v.at[:, core],
+        send_sem=pair_send,
+        recv_sem=pair_recv,
+        device_id=device(0, 1, 0),
+        device_id_type=MESH,
+    )
+    pair.start()
 
     pair.wait()
     half = LIVE // 2
 
     def grad(j, _):
         at = pl.multiple_of(j * half, half)
-        out_v[pl.ds(at, half), :] = dot(
+        grad_ref[pl.ds(at, half), :] = dot(
             cot_v[pl.ds(at, half), :], wall_v[...].reshape(wide, cols), NN
         ).astype(BF16)
-        to = lax.div(j, 2) * SEQ_LEN + SKIP + lax.rem(j, 2) * half
-        pltpu.make_async_copy(
-            out_v.at[pl.ds(at, half)], grad_ref.at[pl.ds(pl.multiple_of(to, 64), half)], out_sem
-        ).start()
         return 0
 
     lax.fori_loop(0, tokens // half, grad, 0)
@@ -338,13 +344,39 @@
         att_ref[:, h * HEAD : (h + 1) * HEAD] = back[h * 16 : (h + 1) * 16]
 
     pltpu.make_async_copy(recv_v.at[pl.ds(1, 63)], recv_v.at[pl.ds(1, 63)], rs_send).wait()
-    pltpu.make_async_copy(xall_v.at[pl.ds(1, 15)], xall_v.at[pl.ds(1, 15)], x_send).wait()
+    pltpu.make_async_copy(xall_v.at[pl.ds(1, 7)], xall_v.at[pl.ds(1, 7)], x_send).wait()
+    x_pair.wait_send()
     pltpu.make_async_copy(wall_v.at[pl.ds(0, 7), 0], wall_v.at[pl.ds(0, 7), 0], w_send).wait()
     for copy in copies:
         copy.wait_send()
-    for copy in zero_copies:
+
+
+def finish(held_ref, nk_ref, nv_ref, att_ref, grad_ref, nk_out, nv_out, att_out, zero_v, sem, zero_sem):
+    seqs = held_ref.shape[0] // LIVE
+    copies = [
+        pltpu.make_async_copy(
+            held_ref.at[pl.ds(s * LIVE, LIVE)],
+            grad_ref.at[pl.ds(s * SEQ_LEN + SKIP, LIVE)],
+            sem.at[s],
+        )
+        for s in range(seqs)
+    ]
+    for copy in copies:
+        copy.start()
+    zero_v[...] = jnp.zeros_like(zero_v)
+    zeros = [
+        pltpu.make_async_copy(zero_v, grad_ref.at[pl.ds(s * SEQ_LEN, SKIP)], zero_sem.at[s])
+        for s in range(seqs)
+    ]
+    for copy in zeros:
+        copy.start()
+    rows_n = nk_out.shape[1]
+    for src, dst in ((nk_ref, nk_out), (nv_ref, nv_out), (att_ref, att_out)):
+        value = src[...].astype(F32)
+        for s in range(dst.shape[0]):
+            dst[s] = value[s * rows_n : (s + 1) * rows_n].astype(BF16)
+    for copy in copies + zeros:
         copy.wait()
-    pltpu.make_async_copy(out_v, out_v, out_sem).wait()
 
 
 def body(*args):
@@ -361,13 +393,13 @@
     grad, new_keys, new_values, attended = pl.pallas_call(
         kernel,
         out_shape=(
-            jax.ShapeDtypeStruct(layer.shape, BF16),
-            jax.ShapeDtypeStruct((n, HEAD), BF16),
-            jax.ShapeDtypeStruct((n, HEAD), BF16),
-            jax.ShapeDtypeStruct((n, QPK * HEAD), BF16),
+            pltpu.VMEM((tokens, cols), BF16),
+            pltpu.VMEM((n, HEAD), BF16),
+            pltpu.VMEM((n, HEAD), BF16),
+            pltpu.VMEM((n, QPK * HEAD), BF16),
         ),
         in_specs=[hbm, hbm, hbm, smem, smem, smem, hbm, hbm, hbm, hbm, hbm, smem],
-        out_specs=(hbm, vmem, vmem, vmem),
+        out_specs=(vmem,) * 4,
         scratch_shapes=[
             pltpu.VMEM((tokens, cols), BF16),
             pltpu.VMEM((tokens, cot.shape[1]), BF16),
@@ -385,12 +417,10 @@
             pltpu.VMEM((4, 2, 128, 128), F32),
             pltpu.VMEM((4, 2, 128, 128), F32),
             pltpu.VMEM((64, n, HEAD), F32),
-            pltpu.VMEM((tokens, cols), BF16),
-            pltpu.VMEM((SKIP, cols), BF16),
             pltpu.VMEM((128, HEAD), F32),
             dma((20,)),
             dma,
-            dma((4,)),
+            dma,
             dma,
             dma,
             dma,
@@ -406,13 +436,25 @@
         compiler_params=pltpu.CompilerParams(
             collective_id=0, has_side_effects=True, vmem_limit_bytes=56 * 1024 * 1024
         ),
-    )(*args)
-    return (
-        grad,
-        new_keys.reshape(steps_n, rows_n, HEAD),
-        new_values.reshape(steps_n, rows_n, HEAD),
-        attended.reshape(steps_n, rows_n, QPK * HEAD),
-    )
+    )(*(pltpu.with_memory_space_constraint(v, pltpu.HBM) if v.dtype == BF16 else v for v in args))
+    held = [pltpu.with_memory_space_constraint(v, pltpu.VMEM) for v in (grad, new_keys, new_values, attended)]
+    return pl.pallas_call(
+        finish,
+        out_shape=(
+            jax.ShapeDtypeStruct(layer.shape, BF16),
+            jax.ShapeDtypeStruct((steps_n, rows_n, HEAD), BF16),
+            jax.ShapeDtypeStruct((steps_n, rows_n, HEAD), BF16),
+            jax.ShapeDtypeStruct((steps_n, rows_n, QPK * HEAD), BF16),
+        ),
+        in_specs=[vmem] * 4,
+        out_specs=(hbm, vmem, vmem, vmem),
+        scratch_shapes=[
+            pltpu.VMEM((SKIP, cols), BF16),
+            dma((seqs,)),
+            dma((seqs,)),
+        ],
+        compiler_params=pltpu.CompilerParams(vmem_limit_bytes=8 * 1024 * 1024),
+    )(*held)
 
 
 def solution(mesh):

time: 48.4 us -> 39 us (0.81)
  local copies, waits for them, and re-layouts: 7.88 us -> 0 us
  Pallas kernels: 39.3 us -> 38.3 us
    unnamed x7 -> x0, local copies, waits for them, and re-layouts: 6.49 us -> none
    reshape x1 -> x0, local copies, waits for them, and re-layouts: 1.39 us -> none  [body(): attended.reshape(steps_n, rows_n, QPK * HEAD)]
    pallas_call x1 -> x2, Pallas kernels: 39.3 us -> 38.3 us  [the longest x1 35.2 us: body(): pl.pallas_call(kernel, out_shape=(pltpu.VMEM((tokens, cols), BF16), pltpu...]
where the time goes in v2:
time: 39 us; the launch traced here: 38.9 us
  Pallas kernels  38.3 us (98%)
  between operations  0.64 us (2%)
    pallas_call x1, Pallas kernels, body(): pl.pallas_call(kernel, out_shape=(pltpu.VMEM((tokens, cols), BF16), pltpu...  35.2 us
    pallas_call x1, Pallas kernels, body(): pl.pallas_call(finish, out_shape=(jax.ShapeDtypeStruct(layer.shape, BF16)...  3.02 us

profile of v2, /device:TPU:1, one launch (start us, length us, event | category | flops | bytes accessed | tf_op | source)
XLA Modules:
  0.0 38.9 jit_solution(17501059493383699031)
XLA Ops:
  0.6 35.2 %shard_map.147 = (bf16[3584,640]{1,0:T(8,128)(2,1)S(1)}, bf16[16,128]{1,0:T(8,128)(2,1)S(1)}, bf16[16,128]{1,0:T(8,128)(2,1)S(1)}, bf16[16,1024]{1,0:T(8,128)(2,1)S(1)}) custom-call(bf16[4096,640]{1,0:T(8,128)(2,1)} %layer_ref.1, bf16[4096,1024]{1,0:T(8,128)(2,1)} %cot_ref.1, bf16[64,640]{1,0:T(8,128)(2,1)} %vw_ref.1, f32[64]{0:T(128)} %rewards_ref.1, ...), custom_call_target="tpu_custom_call" | custom-call | tf_op jit(solution)/shard_map/pallas_call | solution.py:393
  35.9 3.0 %shard_map.148 = (bf16[4096,640]{1,0:T(8,128)(2,1)}, bf16[4,4,128]{2,1,0:T(4,128)(2,1)}, bf16[4,4,128]{2,1,0:T(4,128)(2,1)}, bf16[4,4,1024]{2,1,0:T(4,128)(2,1)}) custom-call(bf16[3584,640]{1,0:T(8,128)(2,1)S(1)} %get-tuple-element.8.held_ref, bf16[16,128]{1,0:T(8,128)(2,1)S(1)} %get-tuple-element.9.nk_ref, bf16[16,128]{1,0:T(8,128)(2,1)S(1)} %get-tuple-element.10.nv_ref, ...), custom_call_target="tpu_custom_call" | custom-call | tf_op jit(solution)/shard_map/pallas_call | solution.py:441

commit v3 on v2

--- a/solution.py
+++ b/solution.py
@@ -49,6 +49,8 @@
     nk_ref,
     nv_ref,
     att_ref,
+    fresh_ref,
+    perm_ref,
     layer_v,
     cot_v,
     vw_v,
@@ -65,7 +67,6 @@
     home_v,
     core_v,
     recv_v,
-    att_v,
     load_sem,
     x_send,
     x_recv,
@@ -85,6 +86,7 @@
     fs = lax.axis_index("fsdp")
     tp = lax.axis_index("tp")
     core = lax.rem(fs, 2)
+    yh = lax.div(fs, 2)
     group = sec * 4 + fs
     seqs = layer_ref.shape[0] // SEQ_LEN
     n_seq = rewards_ref.shape[0]
@@ -147,8 +149,7 @@
     ).astype(BF16)
     xall_v[0] = flat_v[:, pl.ds(pl.multiple_of(tp * cols, 128), cols)]
     vw_load.wait()
-    row_at = sec * 2 + lax.div(fs, 2)
-    wall_v[row_at, core] = vw_v[...]
+    wall_v[sec, yh, core] = vw_v[...]
 
     kw_load.wait()
     new_keys = dot(flat_v[...], kw_v[...], NT).astype(BF16)
@@ -171,9 +172,9 @@
     def send_weight(q):
         pltpu.make_async_remote_copy(
             src_ref=vw_v,
-            dst_ref=wall_v.at[row_at, core],
-            send_sem=w_send,
-            recv_sem=w_recv,
+            dst_ref=wall_v.at[sec, yh, core],
+            send_sem=w_send.at[q % 2],
+            recv_sem=w_recv.at[q % 2],
             device_id=device(q, 0, 0),
             device_id_type=MESH,
         ).start()
@@ -216,9 +217,10 @@
         total = jnp.sum(e, axis=1, keepdims=True) + jnp.sum(fe, axis=1, keepdims=True)
         inv = F32(1.0) / total
         cv_loads[r].wait()
-        att_v[part, :] = dot((e * inv).astype(BF16), cv_v[r], NN)
+        att_ref[part, :] = dot((e * inv).astype(BF16), cv_v[r], NN)
         fresh_probs.append((fe * inv).astype(BF16).astype(F32))
-    fresh_prob = jnp.concatenate(fresh_probs, axis=0).astype(BF16)
+    fresh_ref[...] = jnp.concatenate(fresh_probs, axis=0).astype(BF16)
+    perm_ref[...] = perm
 
     pl.semaphore_wait(ready_sem, 7)
     for q in (5, 3, 7, 1):
@@ -252,17 +254,29 @@
 
     x_pair.wait_recv()
     x_all = xall_v[...].reshape(256, cols)
-    for copy in layer_loads:
-        copy.wait()
     tokens = layer_v.shape[0]
-    blk = 512
-
-    def outer(j, _):
-        at = pl.multiple_of(j * blk, blk)
-        a_v[:, pl.ds(at, blk)] = dot(xall_v[...].reshape(256, cols), layer_v[pl.ds(at, blk), :], NT).astype(BF16)
-        return 0
-
-    lax.fori_loop(0, tokens // blk, outer, 0)
+    blk = LIVE
+
+    for j in range(tokens // blk):
+        layer_loads[j].wait()
+        a_v[:, j * blk : (j + 1) * blk] = dot(x_all, layer_v[j * blk : (j + 1) * blk, :], NT).astype(BF16)
+
+    def pass_on(batch):
+        half_at = flip(yh, batch)
+        n = 3 + batch
+        pltpu.make_async_copy(wall_v.at[pl.ds(0, n), 0, 0], wall_v.at[pl.ds(0, n), 0, 0], w_recv.at[batch]).wait()
+        copy = pltpu.make_async_remote_copy(
+            src_ref=wall_v.at[:, half_at, core],
+            dst_ref=wall_v.at[:, half_at, core],
+            send_sem=pair_send.at[batch],
+            recv_sem=pair_recv.at[batch],
+            device_id=device(0, 1, 0),
+            device_id_type=MESH,
+        )
+        copy.start()
+        return copy
+
+    pairs = [pass_on(0)]
 
     inv_resp = F32(1.0) / responses
     own = dot(x_all, jnp.concatenate([vw_v[...]] * 4, axis=0), NT)
@@ -270,15 +284,15 @@
     own = jnp.where(quarter == lax.rem(group, 4), own, F32(0.0))
     own_chunk = lax.div(group, 4)
     tp_hi, tp_lo = lax.div(tp, 2), lax.rem(tp, 2)
-    copies = []
+    copies = {}
 
     def scatter(k):
         copies[k].wait_recv()
         home_v[k] = home_v[k] + core_v[k]
-        for e in range(2):
+        for e in (0, 1) if k == 1 else (1, 0):
             j = flip(tp_lo, e)
             dt = 2 * k + e
-            for q in range(8):
+            for q in (5, 3, 7, 4, 1, 2, 6, 0):
                 if q or dt:
                     pltpu.make_async_remote_copy(
                         src_ref=home_v.at[k, j, pl.ds(q * 16, 16)],
@@ -291,14 +305,15 @@
         if k == 0:
             recv_v[0] = home_v[0, tp_lo, 0:16, :]
 
-    for k in range(4):
+    last = None
+    for k in (3, 1, 2, 0):
         at = flip(tp_hi, k)
         weighted = cot_v[:, pl.ds(pl.multiple_of(at * 256, 256), 256)]
         part = jnp.where(own_chunk == at, own, F32(0.0)) - dot(a_v[...], weighted, NN) * inv_resp
         for j in range(2):
             home_v[k, j] = part[:128, j * 128 : (j + 1) * 128]
             away_v[k, j] = part[128:, j * 128 : (j + 1) * 128]
-        copy = pltpu.make_async_remote_copy(
+        copies[k] = pltpu.make_async_remote_copy(
             src_ref=away_v.at[k],
             dst_ref=core_v.at[k],
             send_sem=core_send.at[k],
@@ -306,25 +321,16 @@
             device_id=device(0, 1, 0),
             device_id_type=MESH,
         )
-        copy.start()
-        copies.append(copy)
-        if k:
-            scatter(k - 1)
-    scatter(3)
-
-    pltpu.make_async_copy(wall_v.at[pl.ds(0, 7), 0], wall_v.at[pl.ds(0, 7), 0], w_recv).wait()
-    pair = pltpu.make_async_remote_copy(
-        src_ref=wall_v.at[:, core],
-        dst_ref=wall_v.at[:, core],
-        send_sem=pair_send,
-        recv_sem=pair_recv,
-        device_id=device(0, 1, 0),
-        device_id_type=MESH,
-    )
-    pair.start()
-
-    pair.wait()
-    half = LIVE // 2
+        copies[k].start()
+        if last is not None:
+            scatter(last)
+        last = k
+    pairs.append(pass_on(1))
+    scatter(last)
+
+    for copy in pairs:
+        copy.wait()
+    half = 2 * LIVE
 
     def grad(j, _):
         at = pl.multiple_of(j * half, half)
@@ -338,20 +344,17 @@
     pltpu.make_async_copy(recv_v.at[pl.ds(1, 63)], recv_v.at[pl.ds(1, 63)], rs_recv).wait()
     new_values = jnp.sum(recv_v[...], axis=0).astype(BF16)
     nv_ref[...] = new_values
-    done = (att_v[...] + dot(fresh_prob, new_values, NN)).astype(BF16)
-    back = dot(perm, done, (((0,), (0,)), ((), ()))).astype(BF16)
-    for h in range(QPK):
-        att_ref[:, h * HEAD : (h + 1) * HEAD] = back[h * 16 : (h + 1) * 16]
 
     pltpu.make_async_copy(recv_v.at[pl.ds(1, 63)], recv_v.at[pl.ds(1, 63)], rs_send).wait()
     pltpu.make_async_copy(xall_v.at[pl.ds(1, 7)], xall_v.at[pl.ds(1, 7)], x_send).wait()
     x_pair.wait_send()
-    pltpu.make_async_copy(wall_v.at[pl.ds(0, 7), 0], wall_v.at[pl.ds(0, 7), 0], w_send).wait()
-    for copy in copies:
-        copy.wait_send()
-
-
-def finish(held_ref, nk_ref, nv_ref, att_ref, grad_ref, nk_out, nv_out, att_out, zero_v, sem, zero_sem):
+    for n in (3, 4):
+        pltpu.make_async_copy(wall_v.at[pl.ds(0, n), 0, 0], wall_v.at[pl.ds(0, n), 0, 0], w_send.at[n - 3]).wait()
+    for k in range(4):
+        copies[k].wait_send()
+
+
+def finish(held_ref, nk_ref, nv_ref, att_ref, fresh_ref, perm_ref, grad_ref, nk_out, nv_out, att_out, zero_v, sem, zero_sem):
     seqs = held_ref.shape[0] // LIVE
     copies = [
         pltpu.make_async_copy(
@@ -371,8 +374,14 @@
     for copy in zeros:
         copy.start()
     rows_n = nk_out.shape[1]
-    for src, dst in ((nk_ref, nk_out), (nv_ref, nv_out), (att_ref, att_out)):
-        value = src[...].astype(F32)
+    done = (att_ref[...] + dot(fresh_ref[...], nv_ref[...], NN)).astype(BF16)
+    back = dot(perm_ref[...], done, (((0,), (0,)), ((), ())))
+    attended = jnp.concatenate([back[h * 16 : (h + 1) * 16] for h in range(QPK)], axis=1)
+    for value, dst in (
+        (nk_ref[...].astype(F32), nk_out),
+        (nv_ref[...].astype(F32), nv_out),
+        (attended, att_out),
+    ):
         for s in range(dst.shape[0]):
             dst[s] = value[s * rows_n : (s + 1) * rows_n].astype(BF16)
     for copy in copies + zeros:
@@ -390,16 +399,18 @@
     smem = pl.BlockSpec(memory_space=pltpu.SMEM)
     vmem = pl.BlockSpec(memory_space=pltpu.VMEM)
     dma = pltpu.SemaphoreType.DMA
-    grad, new_keys, new_values, attended = pl.pallas_call(
+    results = pl.pallas_call(
         kernel,
         out_shape=(
             pltpu.VMEM((tokens, cols), BF16),
             pltpu.VMEM((n, HEAD), BF16),
             pltpu.VMEM((n, HEAD), BF16),
-            pltpu.VMEM((n, QPK * HEAD), BF16),
+            pltpu.VMEM((n * QPK, HEAD), F32),
+            pltpu.VMEM((n * QPK, n), BF16),
+            pltpu.VMEM((n * QPK, n * QPK), BF16),
         ),
         in_specs=[hbm, hbm, hbm, smem, smem, smem, hbm, hbm, hbm, hbm, hbm, smem],
-        out_specs=(vmem,) * 4,
+        out_specs=(vmem,) * 6,
         scratch_shapes=[
             pltpu.VMEM((tokens, cols), BF16),
             pltpu.VMEM((tokens, cot.shape[1]), BF16),
@@ -411,22 +422,21 @@
             pltpu.VMEM(cv.shape, BF16),
             pltpu.VMEM((n, width), BF16),
             pltpu.VMEM((16, n, cols), BF16),
-            pltpu.VMEM((8, 2, *vw.shape), BF16),
+            pltpu.VMEM((4, 2, 2, *vw.shape), BF16),
             pltpu.VMEM((256, tokens), BF16),
             pltpu.VMEM((4, 2, 128, 128), F32),
             pltpu.VMEM((4, 2, 128, 128), F32),
             pltpu.VMEM((4, 2, 128, 128), F32),
             pltpu.VMEM((64, n, HEAD), F32),
-            pltpu.VMEM((128, HEAD), F32),
             dma((20,)),
             dma,
             dma,
             dma,
             dma,
-            dma,
-            dma,
-            dma,
-            dma,
+            dma((2,)),
+            dma((2,)),
+            dma((2,)),
+            dma((2,)),
             dma((4,)),
             dma((4,)),
             dma,
@@ -437,7 +447,7 @@
             collective_id=0, has_side_effects=True, vmem_limit_bytes=56 * 1024 * 1024
         ),
     )(*(pltpu.with_memory_space_constraint(v, pltpu.HBM) if v.dtype == BF16 else v for v in args))
-    held = [pltpu.with_memory_space_constraint(v, pltpu.VMEM) for v in (grad, new_keys, new_values, attended)]
+    held = [pltpu.with_memory_space_constraint(v, pltpu.VMEM) for v in results]
     return pl.pallas_call(
         finish,
         out_shape=(
@@ -446,7 +456,7 @@
             jax.ShapeDtypeStruct((steps_n, rows_n, HEAD), BF16),
             jax.ShapeDtypeStruct((steps_n, rows_n, QPK * HEAD), BF16),
         ),
-        in_specs=[vmem] * 4,
+        in_specs=[vmem] * 6,
         out_specs=(hbm, vmem, vmem, vmem),
         scratch_shapes=[
             pltpu.VMEM((SKIP, cols), BF16),

time: 39 us -> 35.8 us (0.918)
  Pallas kernels: 38.3 us -> 35.1 us
    pallas_call x1, Pallas kernels: 35.2 us -> 32 us  [body(): pl.pallas_call(kernel, out_shape=(pltpu.VMEM((tokens, cols), BF16), pltpu...]
where the time goes in v3:
time: 35.8 us; the launch traced here: 35.7 us
  Pallas kernels  35.1 us (98%)
  between operations  0.64 us (2%)
    pallas_call x1, Pallas kernels, body(): pl.pallas_call(kernel, out_shape=(pltpu.VMEM((tokens, cols), BF16), pltpu...  32 us
    pallas_call x1, Pallas kernels, body(): pl.pallas_call(finish, out_shape=(jax.ShapeDtypeStruct(layer.shape, BF16)...  3.03 us

profile of v3, /device:TPU:1, one launch (start us, length us, event | category | flops | bytes accessed | tf_op | source)
XLA Modules:
  0.0 35.7 jit_solution(4538058303158146104)
XLA Ops:
  0.6 32.0 %shard_map.147 = (bf16[3584,640]{1,0:T(8,128)(2,1)S(1)}, bf16[16,128]{1,0:T(8,128)(2,1)S(1)}, bf16[16,128]{1,0:T(8,128)(2,1)S(1)}, f32[128,128]{1,0:T(8,128)S(1)...) custom-call(bf16[4096,640]{1,0:T(8,128)(2,1)} %layer_ref.1, bf16[4096,1024]{1,0:T(8,128)(2,1)} %cot_ref.1, ...), custom_call_target="tpu_custom_call" | custom-call | tf_op jit(solution)/shard_map/pallas_call | solution.py:402
  32.7 3.0 %shard_map.148 = (bf16[4096,640]{1,0:T(8,128)(2,1)}, bf16[4,4,128]{2,1,0:T(4,128)(2,1)}, bf16[4,4,128]{2,1,0:T(4,128)(2,1)}, bf16[4,4,1024]{2,1,0:T(4,128)(2,1)}) custom-call(bf16[3584,640]{1,0:T(8,128)(2,1)S(1)} %get-tuple-element.10.held_ref, bf16[16,128]{1,0:T(8,128)(2,1)S(1)} %get-tuple-element.11.nk_ref, bf16[16,128]{1,0:T(8,128)(2,1)S(1)} %get-tuple-element.12.nv_ref, ...), custom_call_target="tpu_custom_call" | custom-call | tf_op jit(solution)/shard_map/pallas_call | solution.py:451

commit v4 on v3

--- a/solution.py
+++ b/solution.py
@@ -51,8 +51,9 @@
     att_ref,
     fresh_ref,
     perm_ref,
+    cot_v,
+    wall_v,
     layer_v,
-    cot_v,
     vw_v,
     step_v,
     query_v,
@@ -61,7 +62,6 @@
     cv_v,
     flat_v,
     xall_v,
-    wall_v,
     a_v,
     away_v,
     home_v,
@@ -102,6 +102,7 @@
     for q in (4, 5, 2, 3, 6, 7, 1):
         pl.semaphore_signal(barrier, inc=1, device_id=device(q, 0, near(q)), device_id_type=MESH)
     pl.semaphore_signal(barrier, inc=1, device_id=device(0, 1, 0), device_id_type=MESH)
+    pl.semaphore_signal(barrier, inc=1, device_id=device(1, 0, 0), device_id_type=MESH)
     for dt in range(1, 8):
         pl.semaphore_signal(barrier, inc=1, device_id=device(0, 0, dt), device_id_type=MESH)
 
@@ -155,7 +156,7 @@
     new_keys = dot(flat_v[...], kw_v[...], NT).astype(BF16)
     nk_ref[...] = new_keys
 
-    pl.semaphore_wait(barrier, 15)
+    pl.semaphore_wait(barrier, 16)
     for q in (4, 5, 2, 3, 6, 7, 1):
         at = pl.multiple_of(flip(tp, near(q)) * cols, 128)
         pltpu.make_async_remote_copy(
@@ -169,18 +170,22 @@
     for dt in range(1, 8):
         pl.semaphore_signal(ready_sem, inc=1, device_id=device(0, 0, dt), device_id_type=MESH)
 
-    def send_weight(q):
+    def send_weight(q, half_at, at):
         pltpu.make_async_remote_copy(
-            src_ref=vw_v,
-            dst_ref=wall_v.at[sec, yh, core],
-            send_sem=w_send.at[q % 2],
-            recv_sem=w_recv.at[q % 2],
+            src_ref=wall_v.at[sec, half_at, core],
+            dst_ref=wall_v.at[sec, half_at, core],
+            send_sem=w_send.at[at],
+            recv_sem=w_recv.at[at],
             device_id=device(q, 0, 0),
             device_id_type=MESH,
         ).start()
 
+    def weight_bytes(n):
+        return wall_v.at[pl.ds(0, n), 0, 0]
+
+    send_weight(1, yh, 2)
     for q in (4, 2, 6):
-        send_weight(q)
+        send_weight(q, yh, 0)
 
     query_load.wait()
     steps_n = query_v.shape[0]
@@ -204,27 +209,22 @@
     fresh_top = jnp.max(fresh, axis=1, keepdims=True)
     slots = ck_v.shape[1]
     slot_at = lax.broadcasted_iota(jnp.int32, (per, slots), 1)
+    for copy in ck_loads + cv_loads:
+        copy.wait()
+    parts = [slice(r * per, (r + 1) * per) for r in range(rows_n)]
+    raw = [dot(queries[parts[r]], ck_v[r], NT) * scale for r in range(rows_n)]
+    raw = [jnp.where(slot_at < len_ref[r], raw[r], F32(-1e30)) for r in range(rows_n)]
+    tops = [jnp.maximum(jnp.max(raw[r], axis=1, keepdims=True), fresh_top[parts[r]]) for r in range(rows_n)]
+    exps = [jnp.exp(raw[r] - tops[r]) for r in range(rows_n)]
+    fresh_exps = [jnp.exp(fresh[parts[r]] - tops[r]) for r in range(rows_n)]
     fresh_probs = []
     for r in range(rows_n):
-        part = slice(r * per, (r + 1) * per)
-        ck_loads[r].wait()
-        scores = dot(queries[part], ck_v[r], NT) * scale
-        live = slot_at < len_ref[r]
-        scores = jnp.where(live, scores, F32(-1e30))
-        top = jnp.maximum(jnp.max(scores, axis=1, keepdims=True), fresh_top[part])
-        e = jnp.where(live, jnp.exp(scores - top), F32(0.0))
-        fe = jnp.where(causal[part], jnp.exp(fresh[part] - top), F32(0.0))
-        total = jnp.sum(e, axis=1, keepdims=True) + jnp.sum(fe, axis=1, keepdims=True)
+        total = jnp.sum(exps[r], axis=1, keepdims=True) + jnp.sum(fresh_exps[r], axis=1, keepdims=True)
         inv = F32(1.0) / total
-        cv_loads[r].wait()
-        att_ref[part, :] = dot((e * inv).astype(BF16), cv_v[r], NN)
-        fresh_probs.append((fe * inv).astype(BF16).astype(F32))
+        att_ref[parts[r], :] = dot((exps[r] * inv).astype(BF16), cv_v[r], NN)
+        fresh_probs.append((fresh_exps[r] * inv).astype(BF16).astype(F32))
     fresh_ref[...] = jnp.concatenate(fresh_probs, axis=0).astype(BF16)
     perm_ref[...] = perm
-
-    pl.semaphore_wait(ready_sem, 7)
-    for q in (5, 3, 7, 1):
-        send_weight(q)
 
     rows_at = lax.broadcasted_iota(jnp.int32, (128, 128), 0)
     wide = cot_v.shape[1]
@@ -252,19 +252,9 @@
 
         lax.fori_loop(0, LIVE // 128, weigh, 0)
 
-    x_pair.wait_recv()
-    x_all = xall_v[...].reshape(256, cols)
-    tokens = layer_v.shape[0]
-    blk = LIVE
-
-    for j in range(tokens // blk):
-        layer_loads[j].wait()
-        a_v[:, j * blk : (j + 1) * blk] = dot(x_all, layer_v[j * blk : (j + 1) * blk, :], NT).astype(BF16)
-
     def pass_on(batch):
         half_at = flip(yh, batch)
-        n = 3 + batch
-        pltpu.make_async_copy(wall_v.at[pl.ds(0, n), 0, 0], wall_v.at[pl.ds(0, n), 0, 0], w_recv.at[batch]).wait()
+        pltpu.make_async_copy(weight_bytes(3), weight_bytes(3), w_recv.at[batch]).wait()
         copy = pltpu.make_async_remote_copy(
             src_ref=wall_v.at[:, half_at, core],
             dst_ref=wall_v.at[:, half_at, core],
@@ -276,19 +266,59 @@
         copy.start()
         return copy
 
-    pairs = [pass_on(0)]
-
     inv_resp = F32(1.0) / responses
-    own = dot(x_all, jnp.concatenate([vw_v[...]] * 4, axis=0), NT)
-    quarter = lax.div(lax.broadcasted_iota(jnp.int32, (256, 256), 1), 64)
-    own = jnp.where(quarter == lax.rem(group, 4), own, F32(0.0))
+    quarter = lax.div(lax.broadcasted_iota(jnp.int32, (128, 256), 1), 64)
     own_chunk = lax.div(group, 4)
     tp_hi, tp_lo = lax.div(tp, 2), lax.rem(tp, 2)
+    vw_four = jnp.concatenate([vw_v[...]] * 4, axis=0)
+
+    def project(side):
+        x = xall_v[side * 8 : side * 8 + 8].reshape(128, cols)
+        for s in range(seqs):
+            if not side:
+                layer_loads[s].wait()
+            span = slice(s * LIVE, (s + 1) * LIVE)
+            a_v[side * 128 : side * 128 + 128, span] = dot(x, layer_v[span, :], NT).astype(BF16)
+        own = dot(x, vw_four, NT)
+        return jnp.where(quarter == lax.rem(group, 4), own, F32(0.0))
+
+    own_home = project(0)
+    pltpu.make_async_copy(weight_bytes(1), weight_bytes(1), w_recv.at[2]).wait()
+    for q in (4, 2, 6):
+        send_weight(q, flip(yh, 1), 1)
+    x_pair.wait_recv()
+    own_away = project(1)
+
+    def partial(side, k, own):
+        at = flip(tp_hi, k)
+        weighted = cot_v[:, pl.ds(pl.multiple_of(at * 256, 256), 256)]
+        a = a_v[side * 128 : side * 128 + 128, :]
+        return jnp.where(own_chunk == at, own, F32(0.0)) - dot(a, weighted, NN) * inv_resp
+
+    order = (3, 1, 2, 0)
     copies = {}
-
-    def scatter(k):
+    for k in order:
+        part = partial(1, k, own_away)
+        for j in range(2):
+            away_v[k, j] = part[:, j * 128 : (j + 1) * 128]
+        copies[k] = pltpu.make_async_remote_copy(
+            src_ref=away_v.at[k],
+            dst_ref=core_v.at[k],
+            send_sem=core_send.at[k],
+            recv_sem=core_recv.at[k],
+            device_id=device(0, 1, 0),
+            device_id_type=MESH,
+        )
+        copies[k].start()
+    pairs = [pass_on(0)]
+    pl.semaphore_wait(ready_sem, 7)
+
+    pairs.append(pass_on(1))
+    for k in order:
+        part = partial(0, k, own_home)
         copies[k].wait_recv()
-        home_v[k] = home_v[k] + core_v[k]
+        for j in range(2):
+            home_v[k, j] = part[:, j * 128 : (j + 1) * 128] + core_v[k, j]
         for e in (0, 1) if k == 1 else (1, 0):
             j = flip(tp_lo, e)
             dt = 2 * k + e
@@ -302,44 +332,16 @@
                         device_id=device(q, 0, dt),
                         device_id_type=MESH,
                     ).start()
-        if k == 0:
-            recv_v[0] = home_v[0, tp_lo, 0:16, :]
-
-    last = None
-    for k in (3, 1, 2, 0):
-        at = flip(tp_hi, k)
-        weighted = cot_v[:, pl.ds(pl.multiple_of(at * 256, 256), 256)]
-        part = jnp.where(own_chunk == at, own, F32(0.0)) - dot(a_v[...], weighted, NN) * inv_resp
-        for j in range(2):
-            home_v[k, j] = part[:128, j * 128 : (j + 1) * 128]
-            away_v[k, j] = part[128:, j * 128 : (j + 1) * 128]
-        copies[k] = pltpu.make_async_remote_copy(
-            src_ref=away_v.at[k],
-            dst_ref=core_v.at[k],
-            send_sem=core_send.at[k],
-            recv_sem=core_recv.at[k],
-            device_id=device(0, 1, 0),
-            device_id_type=MESH,
-        )
-        copies[k].start()
-        if last is not None:
-            scatter(last)
-        last = k
-    pairs.append(pass_on(1))
-    scatter(last)
+    recv_v[0] = home_v[0, tp_lo, 0:16, :]
 
     for copy in pairs:
         copy.wait()
-    half = 2 * LIVE
-
-    def grad(j, _):
-        at = pl.multiple_of(j * half, half)
-        grad_ref[pl.ds(at, half), :] = dot(
-            cot_v[pl.ds(at, half), :], wall_v[...].reshape(wide, cols), NN
-        ).astype(BF16)
-        return 0
-
-    lax.fori_loop(0, tokens // half, grad, 0)
+    wall = wall_v[...].reshape(wide, cols)
+    held = grad_ref.shape[0]
+    blk = held // 2
+    for j in range(held // blk):
+        span = slice(j * blk, (j + 1) * blk)
+        grad_ref[span, :] = dot(cot_v[span, :], wall, NN).astype(BF16)
 
     pltpu.make_async_copy(recv_v.at[pl.ds(1, 63)], recv_v.at[pl.ds(1, 63)], rs_recv).wait()
     new_values = jnp.sum(recv_v[...], axis=0).astype(BF16)
@@ -348,31 +350,55 @@
     pltpu.make_async_copy(recv_v.at[pl.ds(1, 63)], recv_v.at[pl.ds(1, 63)], rs_send).wait()
     pltpu.make_async_copy(xall_v.at[pl.ds(1, 7)], xall_v.at[pl.ds(1, 7)], x_send).wait()
     x_pair.wait_send()
-    for n in (3, 4):
-        pltpu.make_async_copy(wall_v.at[pl.ds(0, n), 0, 0], wall_v.at[pl.ds(0, n), 0, 0], w_send.at[n - 3]).wait()
+    for at, n in enumerate((3, 3, 1)):
+        pltpu.make_async_copy(weight_bytes(n), weight_bytes(n), w_send.at[at]).wait()
     for k in range(4):
         copies[k].wait_send()
 
 
-def finish(held_ref, nk_ref, nv_ref, att_ref, fresh_ref, perm_ref, grad_ref, nk_out, nv_out, att_out, zero_v, sem, zero_sem):
-    seqs = held_ref.shape[0] // LIVE
-    copies = [
-        pltpu.make_async_copy(
-            held_ref.at[pl.ds(s * LIVE, LIVE)],
-            grad_ref.at[pl.ds(s * SEQ_LEN + SKIP, LIVE)],
-            sem.at[s],
-        )
-        for s in range(seqs)
-    ]
-    for copy in copies:
+def finish(
+    held_ref,
+    nk_ref,
+    nv_ref,
+    att_ref,
+    fresh_ref,
+    perm_ref,
+    cot_ref,
+    wall_ref,
+    grad_ref,
+    nk_out,
+    nv_out,
+    att_out,
+    zero_v,
+    last_v,
+    sem,
+    zero_sem,
+):
+    done_n = held_ref.shape[0] // LIVE
+    copies = []
+
+    def write(src, at, rows, to):
+        copy = pltpu.make_async_copy(src.at[pl.ds(at, rows)], grad_ref.at[pl.ds(to, rows)], sem.at[len(copies)])
         copy.start()
+        copies.append(copy)
+
+    for s in range(done_n):
+        write(held_ref, s * LIVE, LIVE, s * SEQ_LEN + SKIP)
     zero_v[...] = jnp.zeros_like(zero_v)
     zeros = [
         pltpu.make_async_copy(zero_v, grad_ref.at[pl.ds(s * SEQ_LEN, SKIP)], zero_sem.at[s])
-        for s in range(seqs)
+        for s in range(done_n + 1)
     ]
     for copy in zeros:
         copy.start()
+    wide = cot_ref.shape[1]
+    wall = wall_ref[...].reshape(wide, held_ref.shape[1])
+    half = LIVE // 2
+    for j in range(2):
+        last_v[j * half : (j + 1) * half, :] = dot(
+            cot_ref[done_n * LIVE + j * half : done_n * LIVE + (j + 1) * half, :], wall, NN
+        ).astype(BF16)
+        write(last_v, j * half, half, done_n * SEQ_LEN + SKIP + j * half)
     rows_n = nk_out.shape[1]
     done = (att_ref[...] + dot(fresh_ref[...], nv_ref[...], NN)).astype(BF16)
     back = dot(perm_ref[...], done, (((0,), (0,)), ((), ())))
@@ -402,18 +428,19 @@
     results = pl.pallas_call(
         kernel,
         out_shape=(
-            pltpu.VMEM((tokens, cols), BF16),
+            pltpu.VMEM((tokens - LIVE, cols), BF16),
             pltpu.VMEM((n, HEAD), BF16),
             pltpu.VMEM((n, HEAD), BF16),
             pltpu.VMEM((n * QPK, HEAD), F32),
             pltpu.VMEM((n * QPK, n), BF16),
             pltpu.VMEM((n * QPK, n * QPK), BF16),
+            pltpu.VMEM((tokens, cot.shape[1]), BF16),
+            pltpu.VMEM((4, 2, 2, *vw.shape), BF16),
         ),
         in_specs=[hbm, hbm, hbm, smem, smem, smem, hbm, hbm, hbm, hbm, hbm, smem],
-        out_specs=(vmem,) * 6,
+        out_specs=(vmem,) * 8,
         scratch_shapes=[
             pltpu.VMEM((tokens, cols), BF16),
-            pltpu.VMEM((tokens, cot.shape[1]), BF16),
             pltpu.VMEM(vw.shape, BF16),
             pltpu.VMEM(step.shape, BF16),
             pltpu.VMEM(query.shape, BF16),
@@ -422,7 +449,6 @@
             pltpu.VMEM(cv.shape, BF16),
             pltpu.VMEM((n, width), BF16),
             pltpu.VMEM((16, n, cols), BF16),
-            pltpu.VMEM((4, 2, 2, *vw.shape), BF16),
             pltpu.VMEM((256, tokens), BF16),
             pltpu.VMEM((4, 2, 128, 128), F32),
             pltpu.VMEM((4, 2, 128, 128), F32),
@@ -433,8 +459,8 @@
             dma,
             dma,
             dma,
-            dma((2,)),
-            dma((2,)),
+            dma((3,)),
+            dma((3,)),
             dma((2,)),
             dma((2,)),
             dma((4,)),
@@ -444,7 +470,7 @@
             pltpu.SemaphoreType.REGULAR,
         ],
         compiler_params=pltpu.CompilerParams(
-            collective_id=0, has_side_effects=True, vmem_limit_bytes=56 * 1024 * 1024
+            collective_id=0, has_side_effects=True, vmem_limit_bytes=46 * 1024 * 1024
         ),
     )(*(pltpu.with_memory_space_constraint(v, pltpu.HBM) if v.dtype == BF16 else v for v in args))
     held = [pltpu.with_memory_space_constraint(v, pltpu.VMEM) for v in results]
@@ -456,11 +482,12 @@
             jax.ShapeDtypeStruct((steps_n, rows_n, HEAD), BF16),
             jax.ShapeDtypeStruct((steps_n, rows_n, QPK * HEAD), BF16),
         ),
-        in_specs=[vmem] * 6,
+        in_specs=[vmem] * 8,
         out_specs=(hbm, vmem, vmem, vmem),
         scratch_shapes=[
             pltpu.VMEM((SKIP, cols), BF16),
-            dma((seqs,)),
+            pltpu.VMEM((LIVE, cols), BF16),
+            dma((seqs + 1,)),
             dma((seqs,)),
         ],
         compiler_params=pltpu.CompilerParams(vmem_limit_bytes=8 * 1024 * 1024),

time: 35.8 us -> 33.7 us (0.941)
  Pallas kernels: 35.1 us -> 32.8 us
    pallas_call x1, Pallas kernels: 32 us -> 29.7 us  [body(): pl.pallas_call(kernel, out_shape=(pltpu.VMEM((tokens - LIVE, cols), BF16)...]
where the time goes in v4:
time: 33.7 us; the launch traced here: 33.5 us
  Pallas kernels  32.8 us (97%)
  between operations  0.64 us (2%)
    pallas_call x1, Pallas kernels, body(): pl.pallas_call(kernel, out_shape=(pltpu.VMEM((tokens - LIVE, cols), BF16)...  29.7 us
    pallas_call x1, Pallas kernels, body(): pl.pallas_call(finish, out_shape=(jax.ShapeDtypeStruct(layer.shape, BF16)...  3.17 us

profile of v4, /device:TPU:1, one launch (start us, length us, event | category | flops | bytes accessed | tf_op | source)
XLA Modules:
  0.0 33.5 jit_solution(10084723497939967866)
XLA Ops:
  0.6 29.7 %shard_map.147 = (bf16[2688,640]{1,0:T(8,128)(2,1)S(1)}, bf16[16,128]{1,0:T(8,128)(2,1)S(1)}, bf16[16,128]{1,0:T(8,128)(2,1)S(1)}, f32[128,128]{1,0:T(8,128)S(1)...) custom-call(bf16[4096,640]{1,0:T(8,128)(2,1)} %layer_ref.1, ...), custom_call_target="tpu_custom_call" | custom-call | tf_op jit(solution)/shard_map/pallas_call | solution.py:428
  30.3 3.2 %shard_map.148 = (bf16[4096,640]{1,0:T(8,128)(2,1)}, bf16[4,4,128]{2,1,0:T(4,128)(2,1)}, bf16[4,4,128]{2,1,0:T(4,128)(2,1)}, bf16[4,4,1024]{2,1,0:T(4,128)(2,1)}) custom-call(bf16[2688,640]{1,0:T(8,128)(2,1)S(1)} %get-tuple-element.12.held_ref, bf16[16,128]{1,0:T(8,128)(2,1)S(1)} %get-tuple-element.13.nk_ref, bf16[16,128]{1,0:T(8,128)(2,1)S(1)} %get-tuple-element.14.nv_ref, ...), custom_call_target="tpu_custom_call" | custom-call | tf_op jit(solution)/shard_map/pallas_call | solution.py:477

commit v5 on v4

--- a/solution.py
+++ b/solution.py
@@ -36,15 +36,15 @@
     layer_ref,
     cot_ref,
     vw_ref,
-    rewards_ref,
-    groups_ref,
-    prompts_ref,
+    rewards_hbm,
+    groups_hbm,
+    prompts_hbm,
     step_ref,
     query_ref,
     kw_ref,
     ck_ref,
     cv_ref,
-    len_ref,
+    len_hbm,
     grad_ref,
     nk_ref,
     nv_ref,
@@ -53,6 +53,10 @@
     perm_ref,
     cot_v,
     wall_v,
+    rewards_ref,
+    groups_ref,
+    prompts_ref,
+    len_ref,
     layer_v,
     vw_v,
     step_v,
@@ -89,11 +93,15 @@
     yh = lax.div(fs, 2)
     group = sec * 4 + fs
     seqs = layer_ref.shape[0] // SEQ_LEN
-    n_seq = rewards_ref.shape[0]
+    n_seq = rewards_hbm.shape[0]
     cols = layer_ref.shape[1]
 
+    secs = [flip(sec, bits) for bits in range(4)]
+    fss = [flip(fs, bits) for bits in range(4)]
+    tps = [flip(tp, bits) for bits in range(8)]
+
     def device(q, dc, dt):
-        return (flip(sec, q // 2), flip(fs, (q % 2) * 2 + dc), flip(tp, dt))
+        return (secs[q // 2], fss[(q % 2) * 2 + dc], tps[dt])
 
     def near(q):
         return 4 * (q % 2)
@@ -113,6 +121,17 @@
 
     step_load = load(step_ref, step_v, 0)
     vw_load = load(vw_ref, vw_v, 1)
+    scalar_loads = [
+        load(src, dst, 20 + at)
+        for at, (src, dst) in enumerate(
+            (
+                (rewards_hbm, rewards_ref),
+                (groups_hbm, groups_ref),
+                (prompts_hbm, prompts_ref),
+                (len_hbm, len_ref),
+            )
+        )
+    ]
     query_load = load(query_ref, query_v, 2)
     kw_load = load(kw_ref, kw_v, 3)
     rows_n = ck_ref.shape[0]
@@ -127,23 +146,6 @@
         for s in range(seqs)
     ]
 
-    first = group * seqs
-    own_groups = [groups_ref[first + s] for s in range(seqs)]
-    own_prompts = [prompts_ref[first + s] for s in range(seqs)]
-
-    def scan(j, carry):
-        prompts = carry[0] + prompts_ref[j]
-        reward = rewards_ref[j]
-        sums = [
-            c + jnp.where(groups_ref[j] == g, reward, F32(0.0))
-            for c, g in zip(carry[1:], own_groups)
-        ]
-        return (prompts, *sums)
-
-    scanned = lax.fori_loop(0, n_seq, scan, (jnp.int32(0),) + (F32(0.0),) * seqs)
-    responses = (n_seq * SEQ_LEN - scanned[0]).astype(F32)
-    advantage = [rewards_ref[first + s] - scanned[1 + s] / F32(GROUP) for s in range(seqs)]
-
     step_load.wait()
     flat_v[...] = jnp.concatenate(
         [step_v[s].astype(F32) for s in range(step_v.shape[0])], axis=0
@@ -186,6 +188,25 @@
     send_weight(1, yh, 2)
     for q in (4, 2, 6):
         send_weight(q, yh, 0)
+
+    for copy in scalar_loads:
+        copy.wait()
+    first = group * seqs
+    own_groups = [groups_ref[first + s] for s in range(seqs)]
+    own_prompts = [prompts_ref[first + s] for s in range(seqs)]
+
+    def scan(j, carry):
+        prompts = carry[0] + prompts_ref[j]
+        reward = rewards_ref[j]
+        sums = [
+            c + jnp.where(groups_ref[j] == g, reward, F32(0.0))
+            for c, g in zip(carry[1:], own_groups)
+        ]
+        return (prompts, *sums)
+
+    scanned = lax.fori_loop(0, n_seq, scan, (jnp.int32(0),) + (F32(0.0),) * seqs)
+    responses = (n_seq * SEQ_LEN - scanned[0]).astype(F32)
+    advantage = [rewards_ref[first + s] - scanned[1 + s] / F32(GROUP) for s in range(seqs)]
 
     query_load.wait()
     steps_n = query_v.shape[0]
@@ -366,6 +387,9 @@
     cot_ref,
     wall_ref,
     grad_ref,
+    nk_hbm,
+    nv_hbm,
+    att_hbm,
     nk_out,
     nv_out,
     att_out,
@@ -373,6 +397,7 @@
     last_v,
     sem,
     zero_sem,
+    small_sem,
 ):
     done_n = held_ref.shape[0] // LIVE
     copies = []
@@ -391,14 +416,6 @@
     ]
     for copy in zeros:
         copy.start()
-    wide = cot_ref.shape[1]
-    wall = wall_ref[...].reshape(wide, held_ref.shape[1])
-    half = LIVE // 2
-    for j in range(2):
-        last_v[j * half : (j + 1) * half, :] = dot(
-            cot_ref[done_n * LIVE + j * half : done_n * LIVE + (j + 1) * half, :], wall, NN
-        ).astype(BF16)
-        write(last_v, j * half, half, done_n * SEQ_LEN + SKIP + j * half)
     rows_n = nk_out.shape[1]
     done = (att_ref[...] + dot(fresh_ref[...], nv_ref[...], NN)).astype(BF16)
     back = dot(perm_ref[...], done, (((0,), (0,)), ((), ())))
@@ -410,7 +427,21 @@
     ):
         for s in range(dst.shape[0]):
             dst[s] = value[s * rows_n : (s + 1) * rows_n].astype(BF16)
-    for copy in copies + zeros:
+    small = [
+        pltpu.make_async_copy(src, dst, small_sem.at[at])
+        for at, (src, dst) in enumerate(((nk_out, nk_hbm), (nv_out, nv_hbm), (att_out, att_hbm)))
+    ]
+    for copy in small:
+        copy.start()
+    wide = cot_ref.shape[1]
+    wall = wall_ref[...].reshape(wide, held_ref.shape[1])
+    half = LIVE // 2
+    for j in range(2):
+        last_v[j * half : (j + 1) * half, :] = dot(
+            cot_ref[done_n * LIVE + j * half : done_n * LIVE + (j + 1) * half, :], wall, NN
+        ).astype(BF16)
+        write(last_v, j * half, half, done_n * SEQ_LEN + SKIP + j * half)
+    for copy in copies + zeros + small:
         copy.wait()
 
 
@@ -422,7 +453,6 @@
     tokens = seqs * LIVE
     cols = layer.shape[1]
     hbm = pl.BlockSpec(memory_space=pl.ANY)
-    smem = pl.BlockSpec(memory_space=pltpu.SMEM)
     vmem = pl.BlockSpec(memory_space=pltpu.VMEM)
     dma = pltpu.SemaphoreType.DMA
     results = pl.pallas_call(
@@ -437,9 +467,13 @@
             pltpu.VMEM((tokens, cot.shape[1]), BF16),
             pltpu.VMEM((4, 2, 2, *vw.shape), BF16),
         ),
-        in_specs=[hbm, hbm, hbm, smem, smem, smem, hbm, hbm, hbm, hbm, hbm, smem],
+        in_specs=[hbm] * 12,
         out_specs=(vmem,) * 8,
         scratch_shapes=[
+            pltpu.SMEM(rewards.shape, F32),
+            pltpu.SMEM(groups.shape, jnp.int32),
+            pltpu.SMEM(prompts.shape, jnp.int32),
+            pltpu.SMEM(lengths.shape, jnp.int32),
             pltpu.VMEM((tokens, cols), BF16),
             pltpu.VMEM(vw.shape, BF16),
             pltpu.VMEM(step.shape, BF16),
@@ -454,7 +488,7 @@
             pltpu.VMEM((4, 2, 128, 128), F32),
             pltpu.VMEM((4, 2, 128, 128), F32),
             pltpu.VMEM((64, n, HEAD), F32),
-            dma((20,)),
+            dma((24,)),
             dma,
             dma,
             dma,
@@ -472,7 +506,7 @@
         compiler_params=pltpu.CompilerParams(
             collective_id=0, has_side_effects=True, vmem_limit_bytes=46 * 1024 * 1024
         ),
-    )(*(pltpu.with_memory_space_constraint(v, pltpu.HBM) if v.dtype == BF16 else v for v in args))
+    )(*(pltpu.with_memory_space_constraint(v, pltpu.HBM) for v in args))
     held = [pltpu.with_memory_space_constraint(v, pltpu.VMEM) for v in results]
     return pl.pallas_call(
         finish,
@@ -483,12 +517,16 @@
             jax.ShapeDtypeStruct((steps_n, rows_n, QPK * HEAD), BF16),
         ),
         in_specs=[vmem] * 8,
-        out_specs=(hbm, vmem, vmem, vmem),
+        out_specs=(hbm,) * 4,
         scratch_shapes=[
+            pltpu.VMEM((steps_n, rows_n, HEAD), BF16),
+            pltpu.VMEM((steps_n, rows_n, HEAD), BF16),
+            pltpu.VMEM((steps_n, rows_n, QPK * HEAD), BF16),
             pltpu.VMEM((SKIP, cols), BF16),
             pltpu.VMEM((LIVE, cols), BF16),
             dma((seqs + 1,)),
             dma((seqs,)),
+            dma((3,)),
         ],
         compiler_params=pltpu.CompilerParams(vmem_limit_bytes=8 * 1024 * 1024),
     )(*held)

time: 33.7 us -> 32.8 us (0.973)
  Pallas kernels: 32.8 us -> 32 us
    pallas_call x1, Pallas kernels: 3.17 us -> 2.66 us  [body(): pl.pallas_call(finish, out_shape=(jax.ShapeDtypeStruct(layer.shape, BF16)...]
where the time goes in v5:
time: 32.8 us; the launch traced here: 32.7 us
  Pallas kernels  32 us (98%)
  between operations  0.64 us (2%)
    pallas_call x1, Pallas kernels, body(): pl.pallas_call(kernel, out_shape=(pltpu.VMEM((tokens - LIVE, cols), BF16)...  29.4 us
    pallas_call x1, Pallas kernels, body(): pl.pallas_call(finish, out_shape=(jax.ShapeDtypeStruct(layer.shape, BF16)...  2.66 us

profile of v5, /device:TPU:1, one launch (start us, length us, event | category | flops | bytes accessed | tf_op | source)
XLA Modules:
  0.0 32.7 jit_solution(16149605078426660049)
XLA Ops:
  0.6 29.4 %shard_map.147 = (bf16[2688,640]{1,0:T(8,128)(2,1)S(1)}, bf16[16,128]{1,0:T(8,128)(2,1)S(1)}, bf16[16,128]{1,0:T(8,128)(2,1)S(1)}, f32[128,128]{1,0:T(8,128)S(1)...) custom-call(bf16[4096,640]{1,0:T(8,128)(2,1)} %layer_ref.1, ...), custom_call_target="tpu_custom_call" | custom-call | tf_op jit(solution)/shard_map/pallas_call | solution.py:458
  30.0 2.7 %shard_map.148 = (bf16[4096,640]{1,0:T(8,128)(2,1)}, bf16[4,4,128]{2,1,0:T(4,128)(2,1)}, bf16[4,4,128]{2,1,0:T(4,128)(2,1)}, bf16[4,4,1024]{2,1,0:T(4,128)(2,1)}) custom-call(bf16[2688,640]{1,0:T(8,128)(2,1)S(1)} %get-tuple-element.12.held_ref, bf16[16,128]{1,0:T(8,128)(2,1)S(1)} %get-tuple-element.13.nk_ref, bf16[16,128]{1,0:T(8,128)(2,1)S(1)} %get-tuple-element.14.nv_ref, ...), custom_call_target="tpu_custom_call" | custom-call | tf_op jit(solution)/shard_map/pallas_call | solution.py:511

commit v6 on v5

--- a/solution.py
+++ b/solution.py
@@ -204,7 +204,9 @@
         ]
         return (prompts, *sums)
 
-    scanned = lax.fori_loop(0, n_seq, scan, (jnp.int32(0),) + (F32(0.0),) * seqs)
+    scanned = (jnp.int32(0),) + (F32(0.0),) * seqs
+    for j in range(n_seq):
+        scanned = scan(j, scanned)
     responses = (n_seq * SEQ_LEN - scanned[0]).astype(F32)
     advantage = [rewards_ref[first + s] - scanned[1 + s] / F32(GROUP) for s in range(seqs)]
 

time: 32.8 us -> 32.5 us (level)
  Pallas kernels: 32 us -> 31.6 us
    pallas_call x1, Pallas kernels: 29.4 us -> 29 us  [body(): pl.pallas_call(kernel, out_shape=(pltpu.VMEM((tokens - LIVE, cols), BF16)...]
where the time goes in v6:
time: 32.5 us; the launch traced here: 32.3 us
  Pallas kernels  31.6 us (97%)
  between operations  0.64 us (2%)
    pallas_call x1, Pallas kernels, body(): pl.pallas_call(kernel, out_shape=(pltpu.VMEM((tokens - LIVE, cols), BF16)...  29 us
    pallas_call x1, Pallas kernels, body(): pl.pallas_call(finish, out_shape=(jax.ShapeDtypeStruct(layer.shape, BF16)...  2.66 us

profile of v6, /device:TPU:1, one launch (start us, length us, event | category | flops | bytes accessed | tf_op | source)
XLA Modules:
  0.0 32.3 jit_solution(2970132421805748414)
XLA Ops:
  0.6 29.0 %shard_map.147 = (bf16[2688,640]{1,0:T(8,128)(2,1)S(1)}, bf16[16,128]{1,0:T(8,128)(2,1)S(1)}, bf16[16,128]{1,0:T(8,128)(2,1)S(1)}, f32[128,128]{1,0:T(8,128)S(1)...) custom-call(bf16[4096,640]{1,0:T(8,128)(2,1)} %layer_ref.1, ...), custom_call_target="tpu_custom_call" | custom-call | tf_op jit(solution)/shard_map/pallas_call | solution.py:460
  29.6 2.7 %shard_map.148 = (bf16[4096,640]{1,0:T(8,128)(2,1)}, bf16[4,4,128]{2,1,0:T(4,128)(2,1)}, bf16[4,4,128]{2,1,0:T(4,128)(2,1)}, bf16[4,4,1024]{2,1,0:T(4,128)(2,1)}) custom-call(bf16[2688,640]{1,0:T(8,128)(2,1)S(1)} %get-tuple-element.12.held_ref, bf16[16,128]{1,0:T(8,128)(2,1)S(1)} %get-tuple-element.13.nk_ref, bf16[16,128]{1,0:T(8,128)(2,1)S(1)} %get-tuple-element.14.nv_ref, ...), custom_call_target="tpu_custom_call" | custom-call | tf_op jit(solution)/shard_map/pallas_call | solution.py:513
